TPU v7x, 512 devices: a whole 4x8x8 slice. The times are simulated.
512 devices in a mesh: batch: 16 (over y, x_lo), feat: 32 (over z, x_hi, core).
Axes of the slice: x: 4 (x_hi: 2, x_lo: 2; x = x_hi * 2 + x_lo), y: 8, z: 8, core: 2. Of those that a mesh axis runs over, the one named last changes fastest.
Arguments:
- view_a: bfloat16 [8192, 4096], P('batch', 'feat')
- view_b: bfloat16 [8192, 4096], P('batch', 'feat')
Outputs:
- grad_a: bfloat16 [8192, 4096], P('batch', 'feat')
- grad_b: bfloat16 [8192, 4096], P('batch', 'feat')
- correlation: float32 [4096, 4096], P('feat', 'batch')
All inputs are finite; a program needn't handle non-finite values.
Results may differ from a plain program's by a relative error of at most 0.0065.
Values may be sent and summed in bfloat16 or wider, within the bound.
A program may use at most 64 MiB of HBM per device.

v0:
```python
import jax
import jax.numpy as jnp
from jax import lax
from jax.sharding import PartitionSpec as P

epsilon = 1e-05
off_weight = 0.0051


def loss_grad(tile, row_start, col_start):
    row_ids = row_start + lax.broadcasted_iota(jnp.int32, tile.shape, 0)
    col_ids = col_start + lax.broadcasted_iota(jnp.int32, tile.shape, 1)
    on_diag = row_ids == col_ids
    return jnp.where(on_diag, -2.0 * (1.0 - tile), 2.0 * off_weight * tile).astype(jnp.bfloat16)


def finish(back, normed, inverse, projected):
    wide_norm = normed.astype(jnp.float32)
    return (inverse * (back - wide_norm * projected)).astype(jnp.bfloat16)


def body(view_a, view_b):
    tok_rows = view_a.shape[0]
    tile_width = view_a.shape[1]
    batch_total = tok_rows * lax.axis_size("batch")
    wide_a = view_a.astype(jnp.float32)
    wide_b = view_b.astype(jnp.float32)
    moment_sums = lax.psum(
        (
            jnp.sum(wide_a, axis=0),
            jnp.sum(wide_a * wide_a, axis=0),
            jnp.sum(wide_b, axis=0),
            jnp.sum(wide_b * wide_b, axis=0),
        ),
        "batch",
    )
    mean_a = moment_sums[0] / batch_total
    inv_a = lax.rsqrt(moment_sums[1] / batch_total - mean_a * mean_a + epsilon)
    mean_b = moment_sums[2] / batch_total
    inv_b = lax.rsqrt(moment_sums[3] / batch_total - mean_b * mean_b + epsilon)
    norm_a = ((wide_a - mean_a) * inv_a).astype(jnp.bfloat16)
    norm_b = ((wide_b - mean_b) * inv_b).astype(jnp.bfloat16)
    full_a, full_b = (
        lax.all_gather(norm_a, "feat", axis=1, tiled=True),
        lax.all_gather(norm_b, "feat", axis=1, tiled=True),
    )
    feat_index = lax.axis_index("feat")
    batch_index = lax.axis_index("batch")
    over_rows = (((0,), (0,)), ((), ()))
    over_cols = (((1,), (1,)), ((), ()))
    part_ab = lax.dot_general(norm_a, full_b, over_rows, preferred_element_type=jnp.float32)
    part_ba = lax.dot_general(norm_b, full_a, over_rows, preferred_element_type=jnp.float32)
    sum_ab, sum_ba = (
        lax.psum_scatter(part_ab, "batch", scatter_dimension=1, tiled=True),
        lax.psum_scatter(part_ba, "batch", scatter_dimension=1, tiled=True),
    )
    correlation = sum_ab / batch_total
    col_start = batch_index * correlation.shape[1]
    grad_tile = loss_grad(correlation, feat_index * tile_width, col_start)
    back_tile = loss_grad(sum_ba / batch_total, feat_index * tile_width, col_start)
    row_strip, trans_strip = (
        lax.all_gather(grad_tile, "batch", axis=1, tiled=True),
        lax.all_gather(back_tile, "batch", axis=1, tiled=True),
    )
    back_b = lax.dot_general(full_a, trans_strip, over_cols, preferred_element_type=jnp.float32)
    back_a = lax.dot_general(full_b, row_strip, over_cols, preferred_element_type=jnp.float32)
    proj_sums = lax.psum(
        (
            jnp.sum(back_a * norm_a.astype(jnp.float32), axis=0),
            jnp.sum(back_b * norm_b.astype(jnp.float32), axis=0),
        ),
        "batch",
    )
    grad_a = finish(back_a, norm_a, inv_a, proj_sums[0] / batch_total)
    grad_b = finish(back_b, norm_b, inv_b, proj_sums[1] / batch_total)
    return (grad_a, grad_b, correlation)


def solution(mesh):
    return jax.shard_map(
        body,
        mesh=mesh,
        in_specs=(P("batch", "feat"), P("batch", "feat")),
        out_specs=(P("batch", "feat"), P("batch", "feat"), P("feat", "batch")),
        check_vma=False,
    )
```

profile of v0, /device:TPU:4, one launch (start us, length us, event | category | flops | bytes accessed | tf_op | source)
XLA Modules:
  0.0 580.0 jit_solution(14785391698856626410)
XLA Ops:
  7.2 0.0 all-gather.9.cloned.1.call-start
  7.2 1.1 convert_reduce_fusion
  8.3 34.7 %all-reduce.1 = (f32[128]{0:T(128)S(1)}, f32[128]{0:T(128)S(1)}, f32[128]{0:T(128)S(1)}, f32[128]{0:T(128)S(1)}) all-reduce(f32[128]{0:T(128)S(1)} %get-tuple-element.6, f32[128]{0:T(128)S(1)} %get-tuple-element.5, f32[128]{0:T(128)S(1)} %get-tuple-element.24, ...), channel_id=1, replica_groups=mesh['batch'=16,'feat'=32] {'batch'}, use_global_device_ids=true, to_apply=%region_7.0 | all-reduce | flops 512 | bytes 4096 | tf_op jit(solution)/shard_map/psum | solution.py:28
  43.0 1.6 fusion.10
  44.6 0.0 all-gather.9.cloned.1.call-update
  44.6 0.0 all-gather.5.cloned.1.call-start
  44.7 1.6 fusion.12
  46.3 0.0 all-gather.5.cloned.1.call-update
  46.3 0.0 copy-start
  46.3 0.0 reduce-scatter.5.cloned.1.call-start
  46.4 91.0 %all-gather.9.cloned.1.call-done = bf16[512,4096]{1,0:T(8,128)(2,1)} async-done(((bf16[512,128]{1,0:T(8,128)(2,1)}), bf16[512,4096]{1,0:T(8,128)(2,1)}) %all-gather.9.cloned.1.call-update) | async-done | bytes 4194320 | tf_op jit(solution)/shard_map/all_gather | solution.py:44
  137.3 4.4 fusion.17
  141.7 0.0 reduce-scatter.5.cloned.1.call-update
  141.8 0.0 copy-start.1
  141.8 0.0 reduce-scatter.3.cloned.1.call-start
  141.8 89.0 %all-gather.5.cloned.1.call-done = bf16[512,4096]{1,0:T(8,128)(2,1)} async-done(((bf16[512,128]{1,0:T(8,128)(2,1)}), bf16[512,4096]{1,0:T(8,128)(2,1)}) %all-gather.5.cloned.1.call-update) | async-done | bytes 4194320 | tf_op jit(solution)/shard_map/all_gather | solution.py:45
  230.9 4.2 fusion.16
  235.1 0.0 reduce-scatter.3.cloned.1.call-update
  235.1 0.0 all-gather.11.cloned.1.call-start
  235.2 74.5 %reduce-scatter.5.cloned.1.call-done = f32[128,256]{1,0:T(8,128)} async-done(((f32[128,4096]{1,0:T(8,128)}), f32[128,256]{1,0:T(8,128)}) %reduce-scatter.5.cloned.1.call-update) | async-done | bytes 131088 | tf_op jit(solution)/shard_map/reduce_scatter | solution.py:55
  309.7 79.6 %reduce-scatter.3.cloned.1.call-done = f32[128,256]{1,0:T(8,128)} async-done(((f32[128,4096]{1,0:T(8,128)}), f32[128,256]{1,0:T(8,128)}) %reduce-scatter.3.cloned.1.call-update) | async-done | bytes 131088 | tf_op jit(solution)/shard_map/reduce_scatter | solution.py:54
  389.4 1.7 fusion.14
  391.1 0.0 all-gather.11.cloned.1.call-update
  391.1 0.0 all-gather.7.cloned.1.call-start
  391.2 0.5 all-gather.7.cloned.1.call-update
  391.7 69.4 %all-gather.11.cloned.1.call-done = bf16[128,4096]{1,0:T(8,128)(2,1)} async-done(((bf16[128,256]{1,0:T(8,128)(2,1)}), bf16[128,4096]{1,0:T(8,128)(2,1)}) %all-gather.11.cloned.1.call-update) | async-done | bytes 1048592 | tf_op jit(solution)/shard_map/all_gather | solution.py:63
  461.1 3.8 fusion.4
  464.9 68.8 %all-gather.7.cloned.1.call-done = bf16[128,4096]{1,0:T(8,128)(2,1)} async-done(((bf16[128,256]{1,0:T(8,128)(2,1)}), bf16[128,4096]{1,0:T(8,128)(2,1)}) %all-gather.7.cloned.1.call-update) | async-done | bytes 1048592 | tf_op jit(solution)/shard_map/all_gather | solution.py:62
  533.7 3.8 fusion
  537.5 34.2 %all-reduce = (f32[128]{0:T(128)S(1)}, f32[128]{0:T(128)S(1)}) all-reduce(f32[128]{0:T(128)S(1)} %get-tuple-element.20, f32[128]{0:T(128)S(1)} %get-tuple-element.22), channel_id=1, replica_groups=mesh['batch'=16,'feat'=32] {'batch'}, use_global_device_ids=true, to_apply=%region_10.11 | all-reduce | flops 256 | bytes 2048 | tf_op jit(solution)/shard_map/psum | solution.py:67
  571.7 0.7 fusion.7
  572.4 0.7 fusion.3
  (12 shorter events, 0.1 us)
Async XLA Ops:
  7.2 130.2 %all-gather.9.cloned.1.call-start = ((), (), s32[]{:S(2)}) async-start(), calls=%async_computation.5 | async-start | bytes 4325376 | tf_op jit(solution)/shard_map/all_gather | solution.py:44
  44.6 186.2 %all-gather.5.cloned.1.call-start = ((), (), s32[]{:S(2)}) async-start(), calls=%async_computation.2 | async-start | bytes 4325376 | tf_op jit(solution)/shard_map/all_gather | solution.py:45
  46.3 184.6 %copy-start = (bf16[512,128]{1,0:T(8,128)(2,1)S(1)}, bf16[512,128]{1,0:T(8,128)(2,1)}, u32[]{:S(2)}) copy-start(bf16[512,128]{1,0:T(8,128)(2,1)} %fusion.10) | copy-start | bytes 393220
  46.3 263.4 %reduce-scatter.5.cloned.1.call-start = ((), (), s32[]{:S(2)}) async-start(), calls=%async_computation.6 | async-start | bytes 2228224 | tf_op jit(solution)/shard_map/reduce_scatter | solution.py:55
  141.8 319.4 %copy-start.1 = (bf16[512,128]{1,0:T(8,128)(2,1)S(1)}, bf16[512,128]{1,0:T(8,128)(2,1)}, u32[]{:S(2)}) copy-start(bf16[512,128]{1,0:T(8,128)(2,1)} %fusion.12) | copy-start | bytes 393220
  141.8 247.6 %reduce-scatter.3.cloned.1.call-start = ((), (), s32[]{:S(2)}) async-start(), calls=%async_computation.3 | async-start | bytes 2228224 | tf_op jit(solution)/shard_map/reduce_scatter | solution.py:54
  235.1 226.0 %all-gather.11.cloned.1.call-start = ((), (), s32[]{:S(2)}) async-start(), calls=%async_computation.7 | async-start | bytes 1114112 | tf_op jit(solution)/shard_map/all_gather | solution.py:63
  391.1 142.6 %all-gather.7.cloned.1.call-start = ((), (), s32[]{:S(2)}) async-start(), calls=%async_computation.4 | async-start | bytes 1114112 | tf_op jit(solution)/shard_map/all_gather | solution.py:62
  464.9 106.8 %copy-start.2 = (bf16[512,128]{1,0:T(8,128)(2,1)S(1)}, bf16[512,128]{1,0:T(8,128)(2,1)}, u32[]{:S(2)}) copy-start(bf16[512,128]{1,0:T(8,128)(2,1)} %param.3) | copy-start | bytes 393220
  464.9 107.5 %copy-start.3 = (bf16[512,128]{1,0:T(8,128)(2,1)S(1)}, bf16[512,128]{1,0:T(8,128)(2,1)}, u32[]{:S(2)}) copy-start(bf16[512,128]{1,0:T(8,128)(2,1)} %param.2) | copy-start | bytes 393220
Sparse Core Ops, SparseCore 0:
  44.7 92.5 all-gather.8
  141.0 89.7 all-gather.4
  233.7 75.9 reduce-scatter.4
  312.4 76.9 reduce-scatter.2
  391.2 69.8 all-gather.10
  463.6 70.1 all-gather.6
where the time goes:
time: 580 us
  waiting for transfers between devices  473 us (82%)
  blocking collectives  68.9 us (12%)
  matrix products  16.2 us (3%)
  between operations  14.2 us (2%)
  other arithmetic  7.43 us (1%)
    all_gather x1, waiting for transfers between devices, body(): lax.all_gather(norm_a, 'feat', axis=1, tiled=True)  91 us
    all_gather x1, waiting for transfers between devices, body(): lax.all_gather(norm_b, 'feat', axis=1, tiled=True)  89 us
    reduce_scatter x1, waiting for transfers between devices, body(): lax.psum_scatter(part_ab, 'batch', scatter_dimension=1, tiled=True)  79.6 us
    reduce_scatter x1, waiting for transfers between devices, body(): lax.psum_scatter(part_ba, 'batch', scatter_dimension=1, tiled=True)  74.5 us
    all_gather x1, waiting for transfers between devices, body(): lax.all_gather(back_tile, 'batch', axis=1, tiled=True)  69.4 us
    all_gather x1, waiting for transfers between devices, body(): lax.all_gather(grad_tile, 'batch', axis=1, tiled=True)  68.8 us
    psum x1, blocking collectives, body(): lax.psum((jnp.sum(wide_a, axis=0), jnp.sum(wide_a * wide_a, axis=0), jnp....  34.7 us
    psum x1, blocking collectives, body(): lax.psum((jnp.sum(back_a * norm_a.astype(jnp.float32), axis=0), jnp.sum(b...  34.2 us
  transfers between devices with their start and end apart: 6, of which 6 were waited for; matrix products, arithmetic and copies ran while one was open for 2% of the time, Pallas kernels for 0%

commit v1 on v0

v1 whole, which is shorter than its diff:
```python
import jax
import jax.numpy as jnp
from jax import lax
from jax.experimental import pallas as pl
from jax.experimental.pallas import tpu as pltpu
from jax.sharding import PartitionSpec as P

MESH = pl.DeviceIdType.MESH
epsilon = 1e-05
off_weight = 0.0051
f32 = jnp.float32
bf16 = jnp.bfloat16


def div(a, n):
    return lax.div(a, jnp.int32(n))


def rem(a, n):
    return lax.rem(a, jnp.int32(n))


def kernel(
    pairs,
    va, vb,
    ga, gb, co,
    stat_own, stats, abuf, bbuf, cpart, csend, crecv, ctile, corrb,
    gbuf, pbuf, asend, bsend, aback, bback,
    bar_unused,
    st_s, st_r, a_s, a_r, b_s, b_r, c_s, c_r, o_s, o_r, g_s, g_r, p_s, p_r, fa_s, fa_r, fb_s, fb_r,
):
    b = lax.axis_index("batch")
    f = lax.axis_index("feat")
    y, l = div(b, 2), rem(b, 2)
    z, h, c = div(f, 4), rem(div(f, 2), 2), rem(f, 2)
    xi = l * 4 + h * 2 + c

    def dev(y_, z_, h_, l_, c_):
        return (y_ * 2 + l_, z_ * 4 + h_ * 2 + c_)

    def ring_dev(y_, z_, xi_):
        return dev(y_, z_, rem(div(xi_, 2), 2), div(xi_, 4), rem(xi_, 2))

    def send(src, dst, s_sem, r_sem, to):
        pltpu.make_async_remote_copy(
            src_ref=src, dst_ref=dst, send_sem=s_sem, recv_sem=r_sem, device_id=to, device_id_type=MESH
        ).start()

    def wait(ref, sem):
        pltpu.make_async_copy(ref, ref, sem).wait()

    def loop(lo, hi, fn):
        def step(i, carry):
            fn(i)
            return carry

        lax.fori_loop(lo, hi, step, 0)

    barrier = pltpu.get_barrier_semaphore()

    def greet(to):
        pl.semaphore_signal(barrier, inc=1, device_id=to, device_id_type=MESH)

    loop(1, 16, lambda e: greet((rem(b + e, 16), f)))
    loop(1, 8, lambda e: greet(ring_dev(y, z, rem(xi + e, 8))))
    loop(1, 8, lambda e: greet(dev(y, rem(z + e, 8), h, l, c)))
    loop(1, 8, lambda e: greet(dev(y, rem(z + e, 8), h, 1 - l, c)))
    y_near = div(y, 2) * 2 + 1 - rem(y, 2)
    loop(0, 8, lambda e: greet(ring_dev(y_near, z, rem(xi + e, 8))))

    wide_a = va[...].astype(f32)
    wide_b = vb[...].astype(f32)
    stat_own[0:1, :] = jnp.sum(wide_a, axis=0, keepdims=True)
    stat_own[1:2, :] = jnp.sum(wide_a * wide_a, axis=0, keepdims=True)
    stat_own[2:3, :] = jnp.sum(wide_b, axis=0, keepdims=True)
    stat_own[3:4, :] = jnp.sum(wide_b * wide_b, axis=0, keepdims=True)
    stat_own[4:8, :] = jnp.zeros((4, 128), f32)
    stats[b] = stat_own[...]

    pl.semaphore_wait(barrier, 15 + 7 + 7 + 7 + 8)

    loop(1, 16, lambda e: send(stat_own, stats.at[b], st_s.at[e], st_r.at[b], (rem(b + e, 16), f)))
    loop(1, 16, lambda e: wait(stats.at[rem(b + e, 16)], st_r.at[rem(b + e, 16)]))
    total = stats[0]
    for i in range(1, 16):
        total = total + stats[i]
    total = total / pairs
    mean_a, mean_b = total[0:1, :], total[2:3, :]
    inv_a = lax.rsqrt(total[1:2, :] - mean_a * mean_a + epsilon)
    inv_b = lax.rsqrt(total[3:4, :] - mean_b * mean_b + epsilon)

    half = rem(z, 2)
    bslot = l * 4 + div(z, 2)
    bbuf[8] = ((vb[...].astype(f32) - mean_b) * inv_b).astype(bf16)
    loop(1, 8, lambda e: send(bbuf.at[8], bbuf.at[bslot], b_s.at[e], b_r.at[bslot], dev(y, rem(z + e, 8), h, half, c)))

    @pl.when(half != l)
    def _():
        send(bbuf.at[8], bbuf.at[bslot], b_s.at[0], b_r.at[bslot], dev(y, z, h, half, c))

    abuf[xi] = ((va[...].astype(f32) - mean_a) * inv_a).astype(bf16)
    loop(
        1, 8,
        lambda e: send(abuf.at[xi], abuf.at[xi], a_s.at[e], a_r.at[xi], ring_dev(y, z, rem(xi + e, 8))),
    )

    @pl.when(half == l)
    def _():
        bbuf[bslot] = bbuf[8]

    loop(1, 8, lambda e: wait(abuf.at[rem(xi + e, 8)], a_r.at[rem(xi + e, 8)]))
    loop(1, 8, lambda e: wait(bbuf.at[rem(bslot + e, 8)], b_r.at[rem(bslot + e, 8)]))

    @pl.when(half != l)
    def _():
        wait(bbuf.at[bslot], b_r.at[bslot])

    def side(buf, k):
        return jnp.concatenate([buf[k * 4 + i] for i in range(4)], axis=1)

    over_rows = (((0,), (0,)), ((), ()))
    over_cols = (((1,), (1,)), ((), ()))
    over_in = (((1,), (0,)), ((), ()))
    whole_a = jnp.concatenate([side(abuf, 0), side(abuf, 1)], axis=0)
    whole_b = jnp.concatenate([side(bbuf, 0), side(bbuf, 1)], axis=0)
    prod = lax.dot_general(whole_a, whole_b, over_rows, preferred_element_type=f32)
    for q in range(4):
        cpart[q] = prod[:, q * 128 : (q + 1) * 128]
    for q in range(4):
        for s in range(2):
            flip = l if s == 0 else 1 - l
            csend[2 * q + flip] = cpart[q, s * 256 : (s + 1) * 256, :].astype(bf16)

    loop(
        1, 8,
        lambda e: send(
            csend.at[rem(y + e, 8)], crecv.at[y], c_s.at[e], c_r.at[y], dev(rem(y + e, 8), z, h, l, c)
        ),
    )
    mine = rem(rem(y, 2) + l, 2)
    q_own = div(y, 2)
    ctile[...] = cpart[q_own, pl.ds(pl.multiple_of(mine * 256, 256), 256), :]
    def add(e):
        frm = rem(y + e, 8)
        wait(crecv.at[frm], c_r.at[frm])
        ctile[...] += crecv[frm].astype(f32)

    loop(1, 8, add)
    corr = ctile[...] / pairs
    ctile[...] = corr

    row_ids = lax.broadcasted_iota(jnp.int32, corr.shape, 0)
    col_ids = lax.broadcasted_iota(jnp.int32, corr.shape, 1)
    here = jnp.where((z == 2 * q_own + l) & (mine == h), c * 128, -100000)
    grad = jnp.where(row_ids == col_ids + here, -2.0 * (1.0 - corr), 2.0 * off_weight * corr).astype(bf16)
    gbuf[y] = grad
    loop(
        1, 8,
        lambda e: send(gbuf.at[y], gbuf.at[y], g_s.at[e], g_r.at[y], dev(rem(y + e, 8), z, h, l, c)),
    )
    both = grad.astype(f32) * corr
    flipped = jnp.sum(both.T, axis=0, keepdims=True)
    pbuf[y, 0:1, :] = jnp.sum(both, axis=0, keepdims=True)
    pbuf[y, 1:2, :] = flipped[:, :128]
    pbuf[y, 2:3, :] = flipped[:, 128:]
    pbuf[y, 3:8, :] = jnp.zeros((5, 128), f32)
    loop(
        1, 8,
        lambda e: send(pbuf.at[y], pbuf.at[y], p_s.at[e], p_r.at[y], dev(rem(y + e, 8), z, h, l, c)),
    )

    y_out = 2 * q_own + l
    at_home = (y_out == y) & (mine == h) & (h == l)
    for k in range(2):
        stay = at_home & (c == k)

        @pl.when(stay)
        def _(k=k):
            corrb[c] = ctile[k * 128 : (k + 1) * 128, :]

        @pl.when(jnp.logical_not(stay))
        def _(k=k):
            send(
                ctile.at[pl.ds(k * 128, 128)], corrb.at[c], o_s.at[k], o_r.at[c], dev(y_out, z, mine, h, jnp.int32(k))
            )

    loop(1, 8, lambda e: wait(gbuf.at[rem(y + e, 8)], g_r.at[rem(y + e, 8)]))
    loop(1, 8, lambda e: wait(pbuf.at[rem(y + e, 8)], p_r.at[rem(y + e, 8)]))

    def grad_cols(q):
        return jnp.concatenate([gbuf[2 * q + l], gbuf[2 * q + 1 - l]], axis=0)

    whole_g = jnp.concatenate([grad_cols(q) for q in range(4)], axis=1)
    proj_b = [pbuf[2 * q, 0:1, :] + pbuf[2 * q + 1, 0:1, :] for q in range(4)]
    proj_a = []
    for i in range(4):
        flip = l if i < 2 else 1 - l
        r = 1 + i % 2
        proj_a.append(sum(pbuf[2 * q + flip, r : r + 1, :] for q in range(4)))

    for k in range(2):
        back = lax.dot_general(side(abuf, k), whole_g, over_in, preferred_element_type=f32)
        for q in range(4):
            bsend[k * 4 + q] = (back[:, q * 128 : (q + 1) * 128] - bbuf[k * 4 + q].astype(f32) * proj_b[q]).astype(bf16)
            to_z = 2 * q + l
            stay = (to_z == z) & (l == k)

            @pl.when(stay)
            def _(k=k, q=q):
                bback[z] = bsend[k * 4 + q]

            @pl.when(jnp.logical_not(stay))
            def _(k=k, q=q, to_z=to_z):
                send(
                    bsend.at[k * 4 + q], bback.at[z], fb_s.at[k * 4 + q], fb_r.at[z], dev(y, to_z, h, jnp.int32(k), c)
                )
    for k in range(2):
        back = lax.dot_general(side(bbuf, k), whole_g, over_cols, preferred_element_type=f32)
        for i in range(4):
            asend[k * 4 + i] = (back[:, i * 128 : (i + 1) * 128] - abuf[k * 4 + i].astype(f32) * proj_a[i]).astype(bf16)
    aback[xi] = asend[xi]
    loop(
        1, 8,
        lambda e: send(
            asend.at[rem(xi + e, 8)], aback.at[xi], fa_s.at[e], fa_r.at[xi], ring_dev(y, z, rem(xi + e, 8))
        ),
    )

    c_from = jnp.where((rem(y, 2) == l) & (h == 0), 1, 0)
    for k in range(2):
        own = (h == l) & (rem(y, 2) == l) & (rem(rem(y, 2) + l, 2) == h) & (c == k)

        @pl.when(jnp.logical_not(own))
        def _(k=k):
            wait(corrb.at[k], o_r.at[k])

        co[:, k * 128 : (k + 1) * 128] = corrb[k]
    del c_from

    loop(1, 8, lambda e: wait(aback.at[rem(xi + e, 8)], fa_r.at[rem(xi + e, 8)]))
    acc = aback[0].astype(f32)
    for i in range(1, 8):
        acc = acc + aback[i].astype(f32)
    ga[...] = (acc * inv_a).astype(bf16)
    loop(1, 8, lambda e: wait(bback.at[rem(z + e, 8)], fb_r.at[rem(z + e, 8)]))

    @pl.when(half != l)
    def _():
        wait(bback.at[z], fb_r.at[z])

    acc = bback[0].astype(f32)
    for i in range(1, 8):
        acc = acc + bback[i].astype(f32)
    gb[...] = (acc * inv_b).astype(bf16)

    loop(1, 16, lambda e: wait(stat_own, st_s.at[e]))
    loop(1, 8, lambda e: wait(bbuf.at[8], b_s.at[e]))

    @pl.when(half != l)
    def _():
        wait(bbuf.at[8], b_s.at[0])

    loop(1, 8, lambda e: wait(abuf.at[xi], a_s.at[e]))
    loop(1, 8, lambda e: wait(csend.at[rem(y + e, 8)], c_s.at[e]))
    loop(1, 8, lambda e: wait(gbuf.at[y], g_s.at[e]))
    loop(1, 8, lambda e: wait(pbuf.at[y], p_s.at[e]))
    loop(1, 8, lambda e: wait(asend.at[rem(xi + e, 8)], fa_s.at[e]))
    for k in range(2):
        @pl.when(jnp.logical_not(at_home & (c == k)))
        def _(k=k):
            wait(ctile.at[pl.ds(k * 128, 128)], o_s.at[k])

        for q in range(4):
            @pl.when(jnp.logical_not((2 * q + l == z) & (l == k)))
            def _(k=k, q=q):
                wait(bsend.at[k * 4 + q], fb_s.at[k * 4 + q])


def body(view_a, view_b):
    rows, cols = view_a.shape
    pairs = rows * lax.axis_size("batch")
    vmem = pl.BlockSpec(memory_space=pltpu.VMEM)
    dma = pltpu.SemaphoreType.DMA

    def call(*args):
        return kernel(float(pairs), *args)

    return pl.pallas_call(
        call,
        name="barlow",
        out_shape=(
            jax.ShapeDtypeStruct((rows, cols), bf16),
            jax.ShapeDtypeStruct((rows, cols), bf16),
            jax.ShapeDtypeStruct((128, 256), f32),
        ),
        in_specs=[vmem, vmem],
        out_specs=(vmem, vmem, vmem),
        scratch_shapes=[
            pltpu.VMEM((8, 128), f32),
            pltpu.VMEM((16, 8, 128), f32),
            pltpu.VMEM((8, rows, 128), bf16),
            pltpu.VMEM((9, rows, 128), bf16),
            pltpu.VMEM((4, 512, 128), f32),
            pltpu.VMEM((8, 256, 128), bf16),
            pltpu.VMEM((8, 256, 128), bf16),
            pltpu.VMEM((256, 128), f32),
            pltpu.VMEM((2, 128, 128), f32),
            pltpu.VMEM((8, 256, 128), bf16),
            pltpu.VMEM((8, 8, 128), f32),
            pltpu.VMEM((8, rows, 128), bf16),
            pltpu.VMEM((8, rows, 128), bf16),
            pltpu.VMEM((8, rows, 128), bf16),
            pltpu.VMEM((8, rows, 128), bf16),
            pltpu.SemaphoreType.REGULAR,
            dma((16,)), dma((16,)),
            dma((8,)), dma((8,)), dma((8,)), dma((8,)), dma((8,)), dma((8,)),
            dma((2,)), dma((2,)), dma((8,)), dma((8,)), dma((8,)), dma((8,)),
            dma((8,)), dma((8,)), dma((8,)), dma((8,)),
        ],
        compiler_params=pltpu.CompilerParams(
            collective_id=0, has_side_effects=True, vmem_limit_bytes=40 * 2**20
        ),
    )(view_a, view_b)


def solution(mesh):
    return jax.shard_map(
        body,
        mesh=mesh,
        in_specs=(P("batch", "feat"), P("batch", "feat")),
        out_specs=(P("batch", "feat"), P("batch", "feat"), P("feat", "batch")),
        check_vma=False,
    )
```

time: 580 us -> 113 us (0.19)
  the two profiles are of different devices: /device:TPU:4 before, /device:TPU:147 now
where the time goes in v1:
time: 113 us
  Pallas kernels  109 us (96%)
  local copies, waits for them, and re-layouts  3.77 us (3%)
    pallas_call x1, Pallas kernels, body(): pl.pallas_call(call, name='barlow', out_shape=(jax.ShapeDtypeStruct((rows...  109 us
    unnamed x7, local copies, waits for them, and re-layouts  3.77 us

profile of v1, /device:TPU:147, one launch (start us, length us, event | category | flops | bytes accessed | tf_op | source)
XLA Modules:
  0.0 113.3 jit_solution(2853719196425467296)
XLA Ops:
  0.6 0.0 copy-start
  0.6 0.9 copy-done
  1.5 0.0 copy-start.1
  1.5 0.9 copy-done.1
  2.4 108.9 %barlow.1 = (bf16[512,128]{1,0:T(8,128)(2,1)S(1)}, bf16[512,128]{1,0:T(8,128)(2,1)S(1)}, f32[128,256]{1,0:T(8,128)S(1)}) custom-call(bf16[512,128]{1,0:T(8,128)(2,1)S(1)} %copy-done, bf16[512,128]{1,0:T(8,128)(2,1)S(1)} %copy-done.1), custom_call_target="tpu_custom_call" | custom-call | tf_op jit(solution)/shard_map/barlow/pallas_call | solution.py:288
  111.3 0.7 copy.8
  112.0 0.7 copy.9
  112.7 0.7 copy.10
Async XLA Ops:
  0.6 0.9 copy-start
  1.5 0.9 copy-start.1

commit v2 on v1

v2 whole, which is shorter than its diff:
```python
import jax
import jax.numpy as jnp
from jax import lax
from jax.experimental import pallas as pl
from jax.experimental.pallas import tpu as pltpu
from jax.sharding import PartitionSpec as P

MESH = pl.DeviceIdType.MESH
epsilon = 1e-05
off_weight = 0.0051
f32 = jnp.float32
bf16 = jnp.bfloat16


def div(a, n):
    return lax.div(a, jnp.int32(n))


def rem(a, n):
    return lax.rem(a, jnp.int32(n))


def kernel(
    pairs,
    va, vb,
    ga, gb, co,
    stat_own, stats, abuf, bbuf, aturn, cwide, cnarrow, crecv, cpass, ctile, corrb,
    gbuf, gfull, bsend, bkeep, bfull, bhalf, bpass, bback, asend, akeep, ain, apass, aback,
    st_s, st_r, a_s, a_r, b_s, b_r, bp_s, c_s, cp_s, cp_r, c_r, o_s, o_r, g_s, gp_r, g_r,
    fb_s, fbp_s, ff_r, fh_r, fb_r, fd_s, fd_r, fa_s, fa_r,
):
    b = lax.axis_index("batch")
    f = lax.axis_index("feat")
    y, l = div(b, 2), rem(b, 2)
    z, h, c = div(f, 4), rem(div(f, 2), 2), rem(f, 2)
    xi = l * 4 + h * 2 + c

    def dev(y_, z_, h_, l_, c_):
        return (y_ * 2 + l_, z_ * 4 + h_ * 2 + c_)

    def ring_dev(y_, z_, xi_):
        return dev(y_, z_, rem(div(xi_, 2), 2), div(xi_, 4), rem(xi_, 2))

    def send(src, dst, s_sem, r_sem, to):
        pltpu.make_async_remote_copy(
            src_ref=src, dst_ref=dst, send_sem=s_sem, recv_sem=r_sem, device_id=to, device_id_type=MESH
        ).start()

    def wait(ref, sem):
        pltpu.make_async_copy(ref, ref, sem).wait()

    def loop(lo, hi, fn):
        def step(i, carry):
            fn(i)
            return carry

        lax.fori_loop(lo, hi, step, 0)

    def corr_to(q):
        return dev(2 * q + l, z, div(y, 4), h, rem(div(y, 2), 2))

    def corr_from(k, p):
        return dev(h * 4 + c * 2 + p, z, l, rem(y, 2), k)

    at_home = (rem(y, 2) == l) & (h == l) & (div(y, 2) == h * 2 + c)

    barrier = pltpu.get_barrier_semaphore()

    def greet(to):
        pl.semaphore_signal(barrier, inc=1, device_id=to, device_id_type=MESH)

    loop(1, 16, lambda e: greet((rem(b + e, 16), f)))
    loop(1, 8, lambda e: greet(ring_dev(y, z, rem(xi + e, 8))))
    loop(1, 8, lambda e: greet(dev(y, rem(z + e, 8), h, l, c)))
    loop(1, 8, lambda e: greet(dev(y, rem(z + e, 8), h, 1 - l, c)))
    for q in range(4):
        @pl.when(jnp.logical_not(at_home & (div(y, 2) == q)))
        def _(q=q):
            greet(corr_to(q))

        @pl.when(jnp.logical_not(at_home & (c == q // 2) & (rem(y, 2) == q % 2)))
        def _(q=q):
            greet(corr_from(q // 2, q % 2))

    wide_a = va[...].astype(f32)
    wide_b = vb[...].astype(f32)
    stat_own[0:1, :] = jnp.sum(wide_a, axis=0, keepdims=True)
    stat_own[1:2, :] = jnp.sum(wide_a * wide_a, axis=0, keepdims=True)
    stat_own[2:3, :] = jnp.sum(wide_b, axis=0, keepdims=True)
    stat_own[3:4, :] = jnp.sum(wide_b * wide_b, axis=0, keepdims=True)
    stat_own[4:8, :] = jnp.zeros((4, 128), f32)
    stats[b] = stat_own[...]

    pl.semaphore_wait(barrier, 15 + 7 + 7 + 7 + 8 - 2 * at_home.astype(jnp.int32))

    loop(1, 16, lambda e: send(stat_own, stats.at[b], st_s, st_r, (rem(b + e, 16), f)))
    wait(stats.at[pl.ds(0, 15)], st_r)
    total = stats[0]
    for i in range(1, 16):
        total = total + stats[i]
    total = total / pairs
    mean_a, mean_b = total[0:1, :], total[2:3, :]
    inv_a = lax.rsqrt(total[1:2, :] - mean_a * mean_a + epsilon)
    inv_b = lax.rsqrt(total[3:4, :] - mean_b * mean_b + epsilon)

    half = rem(z, 2)
    native = half == l
    bslot = l * 4 + div(z, 2)
    bbuf[8] = ((vb[...].astype(f32) - mean_b) * inv_b).astype(bf16)
    for i, d in enumerate((2, 6, 1, 7)):
        send(bbuf.at[8], bbuf.at[bslot], b_s.at[i], b_r.at[bslot], dev(y, rem(z + d, 8), h, half, c))
    abuf[xi] = ((va[...].astype(f32) - mean_a) * inv_a).astype(bf16)
    twin = xi + 1 - 2 * c
    for i, e in enumerate((4, 2, 6)):
        send(abuf.at[xi], abuf.at[xi], a_s.at[i], a_r.at[xi], ring_dev(y, z, rem(xi + e, 8)))
    send(abuf.at[xi], abuf.at[xi], a_s.at[3], a_r.at[xi], ring_dev(y, z, twin))

    @pl.when(jnp.logical_not(native))
    def _():
        send(bbuf.at[8], bbuf.at[bslot], b_s.at[4], b_r.at[bslot], dev(y, z, h, half, c))

    @pl.when(native)
    def _():
        bbuf[bslot] = bbuf[8]
        for p, (frm, one, two) in enumerate(((6, 1, 2), (2, 7, 6))):
            for k in range(2):
                slot = k * 4 + div(rem(z + frm, 8), 2)
                wait(bbuf.at[slot], b_r.at[slot])
                send(bbuf.at[slot], bbuf.at[slot], bp_s.at[p, k, 0], b_r.at[slot], dev(y, rem(z + one, 8), h, l, c))
                part = bbuf.at[slot, pl.ds(p * 256, 256)]
                send(part, part, bp_s.at[p, k, 1], b_r.at[slot], dev(y, rem(z + two, 8), h, l, c))

    def turn(slot):
        aturn[rem(slot, 4), :, pl.ds(pl.multiple_of(div(slot, 4) * 512, 512), 512)] = abuf[slot].T

    turn(xi)
    for i, e in enumerate((2, 6, 4)):
        slot = rem(xi + e, 8)
        wait(abuf.at[slot], a_r.at[slot])
        send(abuf.at[slot], abuf.at[slot], a_s.at[4 + i], a_r.at[slot], ring_dev(y, z, twin))
        turn(slot)
    for e in (0, 2, 6, 4):
        slot = rem(twin + e, 8)
        wait(abuf.at[slot], a_r.at[slot])
        turn(slot)

    def side(buf, k):
        return jnp.concatenate([buf[k * 4 + i] for i in range(4)], axis=1)

    over_cols = (((1,), (1,)), ((), ()))
    over_in = (((1,), (0,)), ((), ()))

    def block(t):
        ahead = jnp.where(native, (2, 6, 4, 0)[t], (3, 5, 1, 7)[t])
        return div(rem(z + ahead, 8), 2)

    def along_y(e):
        return dev(rem(y + e, 8), z, h, l, c)

    def rows_of(to):
        return pl.ds(pl.multiple_of(to * 64, 64), 64)

    def correlate(t):
        q = block(t)
        for k in range(2):
            if t < 2:
                @pl.when(jnp.logical_not(native))
                def _(k=k):
                    wait(bbuf.at[k * 4 + q], b_r.at[k * 4 + q])
            elif t == 2:
                wait(bbuf.at[k * 4 + q], b_r.at[k * 4 + q])
            else:
                @pl.when(jnp.logical_not(native & (l == k)))
                def _(k=k):
                    wait(bbuf.at[k * 4 + q], b_r.at[k * 4 + q])

        right = jnp.concatenate([bbuf[q], bbuf[4 + q]], axis=0)
        left = jnp.concatenate([aturn[i] for i in range(4)], axis=0)
        part = lax.dot_general(left, right, over_in, preferred_element_type=f32)
        cwide[t] = part
        cnarrow[t] = part.astype(bf16)

        def go(e, to, slot, sem, lo=0, n=64):
            piece = cnarrow.at[t, pl.ds(pl.multiple_of(rem(y + e, 8) * 64 + lo, 32), n)]
            send(piece, crecv.at[t, slot, pl.ds(lo, n)], c_s.at[t], sem, along_y(to))

        go(3, 1, 2, cp_r.at[t])
        go(5, 7, 3, cp_r.at[t])
        go(4, 6, 4, cp_r.at[t], 0, 32)
        go(4, 2, 5, cp_r.at[t], 32, 32)
        go(1, 1, 0, c_r.at[t])
        go(7, 7, 1, c_r.at[t])

    def pass_partial(t):
        wait(crecv.at[t, pl.ds(0, 3)], cp_r.at[t])
        up = cwide[t, rows_of(rem(y + 2, 8)), :] + crecv[t, 2].astype(f32)
        cpass[t, 0, 0:32, :] = up[:32].astype(bf16)
        cpass[t, 0, 32:64, :] = (up[32:] + crecv[t, 5, 32:64, :].astype(f32)).astype(bf16)
        send(cpass.at[t, 0], crecv.at[t, 6], cp_s.at[t], c_r.at[t], along_y(2))
        down = cwide[t, rows_of(rem(y + 6, 8)), :] + crecv[t, 3].astype(f32)
        cpass[t, 1, 0:32, :] = (down[:32] + crecv[t, 4, 0:32, :].astype(f32)).astype(bf16)
        cpass[t, 1, 32:64, :] = down[32:].astype(bf16)
        send(cpass.at[t, 1], crecv.at[t, 7], cp_s.at[t], c_r.at[t], along_y(6))

    def differentiate(t):
        q = block(t)
        wait(crecv.at[t, pl.ds(0, 4)], c_r.at[t])
        corr = cwide[t, rows_of(y), :]
        for i in (0, 1, 6, 7):
            corr = corr + crecv[t, i].astype(f32)
        corr = corr / pairs
        ctile[q] = corr
        row_ids = lax.broadcasted_iota(jnp.int32, corr.shape, 0)
        col_ids = lax.broadcasted_iota(jnp.int32, corr.shape, 1)
        here = jnp.where((z == 2 * q + l) & (div(y, 2) == h * 2 + c), rem(y, 2) * 64, 100000)
        grad = jnp.where(row_ids + here == col_ids, -2.0 * (1.0 - corr), 2.0 * off_weight * corr).astype(bf16)
        both = grad.astype(f32) * corr
        cols = jnp.sum(both, axis=0, keepdims=True)
        rows = jnp.sum(both.T, axis=0, keepdims=True)
        none = jnp.zeros_like(rows)
        rows = jnp.where(
            rem(y, 2) == 0, jnp.concatenate([rows, none], axis=1), jnp.concatenate([none, rows], axis=1)
        )
        terms = []
        for value in (cols, rows):
            high = value.astype(bf16).astype(f32)
            terms += [high, value - high]
        terms.append(jnp.zeros((12, 128), f32))
        gbuf[q, y, 0:64, :] = grad
        gbuf[q, y, 64:80, :] = jnp.concatenate(terms, axis=0).astype(bf16)
        send(gbuf.at[q, y], gbuf.at[q, y], g_s.at[t], gp_r.at[t], along_y(2))
        send(gbuf.at[q, y], gbuf.at[q, y], g_s.at[t], gp_r.at[t], along_y(6))
        send(gbuf.at[q, y], gbuf.at[q, y], g_s.at[t], g_r.at[t], along_y(1))
        send(gbuf.at[q, y], gbuf.at[q, y], g_s.at[t], g_r.at[t], along_y(7))

    def pass_gradient(t):
        q = block(t)
        wait(gbuf.at[q, pl.ds(0, 2)], gp_r.at[t])
        for frm, one, two, lo, n in ((6, 1, 2, 0, 48), (2, 7, 6, 48, 32)):
            item = gbuf.at[q, rem(y + frm, 8)]
            send(item, item, g_s.at[t], g_r.at[t], along_y(one))
            part = gbuf.at[q, rem(y + frm, 8), pl.ds(lo, n)]
            send(part, part, g_s.at[t], g_r.at[t], along_y(two))

    proj_a = [jnp.zeros((1, 128), f32)] * 4
    proj_b = []

    def take_gradient(t):
        q = block(t)
        wait(gbuf.at[q, pl.ds(0, 5)], g_r.at[t])
        total = jnp.zeros((1, 128), f32)
        for i in range(8):
            gfull[q, i * 64 : (i + 1) * 64, :] = gbuf[q, i, 0:64, :]
            sums = gbuf[q, i, 64:80, :].astype(f32)
            total = total + (sums[0:1, :] + sums[1:2, :])
            proj_a[i // 2] = proj_a[i // 2] + (sums[2:3, :] + sums[3:4, :])
        proj_b.append(total)

    def in_column(d):
        return dev(y, rem(z + d, 8), h, l, c)

    def back_columns(t):
        q = block(t)
        for k in range(2):
            back = lax.dot_general(side(abuf, k), gfull[q], over_in, preferred_element_type=f32)
            back = back - bbuf[k * 4 + q].astype(f32) * proj_b[t]
            if t < 2:
                bkeep[t, k] = back
            bsend[t, k] = back.astype(bf16)

            if t < 2:
                @pl.when(jnp.logical_not(native))
                def _(k=k):
                    send(bsend.at[t, k], bfull.at[t, k], fb_s.at[t, k], ff_r.at[t, k], in_column((1, 7)[t]))
            elif t == 2:
                @pl.when(native)
                def _(k=k):
                    for p, d in enumerate((2, 6)):
                        rows = pl.ds(256 - p * 256, 256)
                        send(
                            bsend.at[t, k, rows], bhalf.at[p, k, rows], fb_s.at[t, k], fh_r.at[p, k], in_column(d)
                        )

                @pl.when(jnp.logical_not(native))
                def _(k=k):
                    send(
                        bsend.at[t, k], bback.at[0], fb_s.at[t, k], fb_r.at[0], dev(y, rem(z + 1, 8), h, jnp.int32(k), c)
                    )
            else:
                @pl.when(native & (l == k))
                def _(k=k):
                    bback[4] = bsend[t, k]

                @pl.when(native & (l != k))
                def _(k=k):
                    send(bsend.at[t, k], bback.at[4], fb_s.at[t, k], fb_r.at[4], dev(y, z, h, jnp.int32(k), c))

                @pl.when(jnp.logical_not(native))
                def _(k=k):
                    send(
                        bsend.at[t, k], bback.at[1], fb_s.at[t, k], fb_r.at[1], dev(y, rem(z + 7, 8), h, jnp.int32(k), c)
                    )

    def pass_back():
        for p, d in enumerate((2, 6)):
            for k in range(2):
                rows = pl.ds(256 - p * 256, 256)
                wait(bfull.at[p, k], ff_r.at[p, k])
                wait(bhalf.at[p, k, rows], fh_r.at[p, k])
                one = slice(256 - p * 256, 512 - p * 256)
                other = slice(p * 256, 256 + p * 256)
                bpass[p, k, other, :] = (bkeep[p, k, other, :] + bfull[p, k, other, :].astype(f32)).astype(bf16)
                bpass[p, k, one, :] = (
                    bkeep[p, k, one, :] + bfull[p, k, one, :].astype(f32) + bhalf[p, k, one, :].astype(f32)
                ).astype(bf16)
                send(
                    bpass.at[p, k], bback.at[2 + p], fbp_s.at[p, k], fb_r.at[2 + p],
                    dev(y, rem(z + d, 8), h, jnp.int32(k), c),
                )

    correlate(0)
    correlate(1)
    pass_partial(0)
    correlate(2)
    pass_partial(1)
    differentiate(0)
    correlate(3)
    pass_partial(2)
    differentiate(1)
    pass_gradient(0)
    pass_partial(3)
    differentiate(2)
    pass_gradient(1)
    take_gradient(0)
    back_columns(0)
    differentiate(3)
    pass_gradient(2)
    take_gradient(1)
    back_columns(1)
    pass_gradient(3)
    take_gradient(2)
    back_columns(2)

    for q in range(4):
        stay = at_home & (div(y, 2) == q)

        @pl.when(stay)
        def _(q=q):
            corrb[c, rem(y, 2)] = ctile[q]

        @pl.when(jnp.logical_not(stay))
        def _(q=q):
            send(ctile.at[q], corrb.at[c, rem(y, 2)], o_s.at[q], o_r.at[c, rem(y, 2)], corr_to(q))

    take_gradient(3)
    whole_g = jnp.concatenate([gfull[q] for q in range(4)], axis=1)
    for k in range(2):
        back = lax.dot_general(side(bbuf, k), whole_g, over_cols, preferred_element_type=f32)
        for i in range(4):
            less = back[:, i * 128 : (i + 1) * 128] - abuf[k * 4 + i].astype(f32) * proj_a[i]
            akeep[k * 4 + i] = less
            asend[k * 4 + i] = less.astype(bf16)
    chip = l * 2 + h
    for e in (2, 1, 3, 0):
        to = rem(chip + e, 4)
        send(asend.at[to * 2 + 1 - c], ain.at[to], fd_s.at[e], fd_r.at[to], ring_dev(y, z, twin))

    back_columns(3)

    for e in (2, 1, 3, 0):
        to = rem(chip + e, 4)
        wait(ain.at[to], fd_r.at[to])
        summed = (akeep[to * 2 + c] + ain[to].astype(f32)).astype(bf16)
        if e:
            apass[e] = summed
            send(apass.at[e], aback.at[chip], fa_s.at[e], fa_r.at[chip], ring_dev(y, z, to * 2 + c))
        else:
            aback[chip] = summed

    @pl.when(native)
    def _():
        pass_back()

    for k in range(2):
        for p in range(2):
            @pl.when(jnp.logical_not(at_home & (c == k) & (rem(y, 2) == p)))
            def _(k=k, p=p):
                wait(corrb.at[k, p], o_r.at[k, p])

            co[p * 64 : (p + 1) * 64, k * 128 : (k + 1) * 128] = corrb[k, p]

    for i in range(4):
        wait(bback.at[i], fb_r.at[i])

    @pl.when(jnp.logical_not(native))
    def _():
        wait(bback.at[4], fb_r.at[4])

    acc = bback[0].astype(f32)
    for i in range(1, 5):
        acc = acc + bback[i].astype(f32)
    gb[...] = (acc * inv_b).astype(bf16)

    for e in range(1, 4):
        frm = rem(chip + e, 4)
        wait(aback.at[frm], fa_r.at[frm])
    acc = aback[0].astype(f32)
    for i in range(1, 4):
        acc = acc + aback[i].astype(f32)
    ga[...] = (acc * inv_a).astype(bf16)

    wait(stats.at[pl.ds(0, 15)], st_s)
    for i in range(4):
        wait(bbuf.at[8], b_s.at[i])
    for i in range(7):
        wait(abuf.at[xi], a_s.at[i])
    for e in range(4):
        wait(asend.at[0], fd_s.at[e])
        if e:
            wait(apass.at[e], fa_s.at[e])

    @pl.when(jnp.logical_not(native))
    def _():
        wait(bbuf.at[8], b_s.at[4])

    @pl.when(native)
    def _():
        for p in range(2):
            for k in range(2):
                wait(bbuf.at[8], bp_s.at[p, k, 0])
                wait(bbuf.at[8, pl.ds(0, 256)], bp_s.at[p, k, 1])
                wait(bpass.at[p, k], fbp_s.at[p, k])

    for t in range(4):
        wait(crecv.at[t, pl.ds(0, 5)], c_s.at[t])
        wait(crecv.at[t, pl.ds(0, 2)], cp_s.at[t])
        wait(gbuf.at[t, pl.ds(0, 7)], g_s.at[t])

        @pl.when(jnp.logical_not(at_home & (div(y, 2) == t)))
        def _(t=t):
            wait(ctile.at[t], o_s.at[t])

        for k in range(2):
            @pl.when((jnp.logical_not(native)) | (t == 2) | ((t == 3) & (l != k)))
            def _(k=k, t=t):
                wait(bsend.at[t, k], fb_s.at[t, k])


def body(view_a, view_b):
    rows, cols = view_a.shape
    pairs = rows * lax.axis_size("batch")
    vmem = pl.BlockSpec(memory_space=pltpu.VMEM)
    dma = pltpu.SemaphoreType.DMA

    def call(*args):
        return kernel(float(pairs), *args)

    return pl.pallas_call(
        call,
        name="barlow",
        out_shape=(
            jax.ShapeDtypeStruct((rows, cols), bf16),
            jax.ShapeDtypeStruct((rows, cols), bf16),
            jax.ShapeDtypeStruct((128, 256), f32),
        ),
        in_specs=[vmem, vmem],
        out_specs=(vmem, vmem, vmem),
        scratch_shapes=[
            pltpu.VMEM((8, 128), f32),
            pltpu.VMEM((16, 8, 128), f32),
            pltpu.VMEM((8, rows, 128), bf16),
            pltpu.VMEM((9, rows, 128), bf16),
            pltpu.VMEM((4, 128, 1024), bf16),
            pltpu.VMEM((4, 512, 128), f32),
            pltpu.VMEM((4, 512, 128), bf16),
            pltpu.VMEM((4, 8, 64, 128), bf16),
            pltpu.VMEM((4, 2, 64, 128), bf16),
            pltpu.VMEM((4, 64, 128), f32),
            pltpu.VMEM((2, 2, 64, 128), f32),
            pltpu.VMEM((4, 8, 80, 128), bf16),
            pltpu.VMEM((4, 512, 128), bf16),
            pltpu.VMEM((4, 2, rows, 128), bf16),
            pltpu.VMEM((2, 2, rows, 128), f32),
            pltpu.VMEM((2, 2, rows, 128), bf16),
            pltpu.VMEM((2, 2, rows, 128), bf16),
            pltpu.VMEM((2, 2, rows, 128), bf16),
            pltpu.VMEM((5, rows, 128), bf16),
            pltpu.VMEM((8, rows, 128), bf16),
            pltpu.VMEM((8, rows, 128), f32),
            pltpu.VMEM((4, rows, 128), bf16),
            pltpu.VMEM((4, rows, 128), bf16),
            pltpu.VMEM((4, rows, 128), bf16),
            dma, dma,
            dma((7,)), dma((8,)), dma((5,)), dma((8,)), dma((2, 2, 2)),
            dma((4,)), dma((4,)), dma((4,)), dma((4,)), dma((4,)), dma((2, 2)), dma((4,)), dma((4,)), dma((4,)),
            dma((4, 2)), dma((2, 2)), dma((2, 2)), dma((2, 2)), dma((5,)),
            dma((4,)), dma((4,)), dma((4,)), dma((4,)),
        ],
        compiler_params=pltpu.CompilerParams(
            collective_id=0, has_side_effects=True, vmem_limit_bytes=40 * 2**20
        ),
    )(view_a, view_b)


def solution(mesh):
    return jax.shard_map(
        body,
        mesh=mesh,
        in_specs=(P("batch", "feat"), P("batch", "feat")),
        out_specs=(P("batch", "feat"), P("batch", "feat"), P("feat", "batch")),
        check_vma=False,
    )
```

time: 113 us -> 88.2 us (0.78)
  the two profiles are of different devices: /device:TPU:147 before, /device:TPU:16 now
where the time goes in v2:
time: 88.2 us; the launch traced here: 88.1 us
  Pallas kernels  83.7 us (95%)
  local copies, waits for them, and re-layouts  3.77 us (4%)
    pallas_call x1, Pallas kernels, body(): pl.pallas_call(call, name='barlow', out_shape=(jax.ShapeDtypeStruct((rows...  83.7 us
    unnamed x7, local copies, waits for them, and re-layouts  3.77 us

profile of v2, /device:TPU:16, one launch (start us, length us, event | category | flops | bytes accessed | tf_op | source)
XLA Modules:
  0.0 88.1 jit_solution(13351710933714099283)
XLA Ops:
  0.6 0.0 copy-start
  0.6 0.9 %copy-done = bf16[512,128]{1,0:T(8,128)(2,1)S(1)} copy-done((bf16[512,128]{1,0:T(8,128)(2,1)S(1)}, bf16[512,128]{1,0:T(8,128)(2,1)}, u32[]{:S(2)}) %copy-start) | copy-done | bytes 131096
  1.5 0.0 copy-start.1
  1.5 0.9 %copy-done.1 = bf16[512,128]{1,0:T(8,128)(2,1)S(1)} copy-done((bf16[512,128]{1,0:T(8,128)(2,1)S(1)}, bf16[512,128]{1,0:T(8,128)(2,1)}, u32[]{:S(2)}) %copy-start.1) | copy-done | bytes 131096
  2.4 83.7 %barlow.1 = (bf16[512,128]{1,0:T(8,128)(2,1)S(1)}, bf16[512,128]{1,0:T(8,128)(2,1)S(1)}, f32[128,256]{1,0:T(8,128)S(1)}) custom-call(bf16[512,128]{1,0:T(8,128)(2,1)S(1)} %copy-done, bf16[512,128]{1,0:T(8,128)(2,1)S(1)} %copy-done.1), custom_call_target="tpu_custom_call" | custom-call | tf_op jit(solution)/shard_map/barlow/pallas_call | solution.py:458
  86.1 0.7 copy.8
  86.8 0.7 copy.9
  87.4 0.7 copy.10
Async XLA Ops:
  0.6 0.9 %copy-start = (bf16[512,128]{1,0:T(8,128)(2,1)S(1)}, bf16[512,128]{1,0:T(8,128)(2,1)}, u32[]{:S(2)}) copy-start(bf16[512,128]{1,0:T(8,128)(2,1)} %args_0_.4) | copy-start | bytes 393220
  1.5 0.9 %copy-start.1 = (bf16[512,128]{1,0:T(8,128)(2,1)S(1)}, bf16[512,128]{1,0:T(8,128)(2,1)}, u32[]{:S(2)}) copy-start(bf16[512,128]{1,0:T(8,128)(2,1)} %args_1_.4) | copy-start | bytes 393220

commit v3 on v2

--- a/solution.py
+++ b/solution.py
@@ -20,14 +20,18 @@
     return lax.rem(a, jnp.int32(n))
 
 
+offs_on = ((0, 1), (2, 3), (4, 5), (6, 7))
+offs_off = ((7, 0), (5, 6), (3, 4), (1, 2))
+
+
 def kernel(
     pairs,
     va, vb,
     ga, gb, co,
-    stat_own, stats, abuf, bbuf, aturn, cwide, cnarrow, crecv, cpass, ctile, corrb,
-    gbuf, gfull, bsend, bkeep, bfull, bhalf, bpass, bback, asend, akeep, ain, apass, aback,
-    st_s, st_r, a_s, a_r, b_s, b_r, bp_s, c_s, cp_s, cp_r, c_r, o_s, o_r, g_s, gp_r, g_r,
-    fb_s, fbp_s, ff_r, fh_r, fb_r, fd_s, fd_r, fa_s, fa_r,
+    stat_own, stats, astat, bstat, abuf, bbuf, anorm, bnorm, aturn, cwide, cnarrow, crecv, cpass, ctile, corrb,
+    gbuf, gfull, bsend, bkeep, bfull, bhalf, bpass, bback, bown, bcross, asend, akeep, ain, apass, aback,
+    st_s, st_r, ms_s, as_r, bs_r, a_s, a_r, b_s, b_r, bp_s, c_s, cp_s, cp_r, c_r, o_s, o_r, g_s, gp_r, g_r,
+    fb_s, fbp_s, ff_r, fh_r, fb_r, fd_s, fd_r, fa_s, fa_r, bx_r, bx_s, bc_r, bc_s,
 ):
     b = lax.axis_index("batch")
     f = lax.axis_index("feat")
@@ -94,6 +98,48 @@
     pl.semaphore_wait(barrier, 15 + 7 + 7 + 7 + 8 - 2 * at_home.astype(jnp.int32))
 
     loop(1, 16, lambda e: send(stat_own, stats.at[b], st_s, st_r, (rem(b + e, 16), f)))
+
+    half = rem(z, 2)
+    native = half == l
+    twin = xi + 1 - 2 * c
+
+    def in_column(d):
+        return dev(y, rem(z + d, 8), h, l, c)
+
+    def slot_at(d):
+        place = rem(z + d, 8)
+        on = rem(rem(place, 2) + l + 1, 2)
+        return (on * l + (1 - on) * (1 - l)) * 4 + div(rem(place + 7 + on, 8), 2)
+
+    def spread_b():
+        slot = slot_at(0)
+        for i, d in enumerate((2, 6, 1, 7)):
+            send(bbuf.at[slot], bbuf.at[slot], b_s.at[i], b_r.at[slot], in_column(d))
+
+    def pass_b():
+        for p, (frm, one, two) in enumerate(((6, 1, 2), (2, 7, 6))):
+            slot = slot_at(frm)
+            wait(bbuf.at[slot], b_r.at[slot])
+            send(bbuf.at[slot], bbuf.at[slot], bp_s.at[p, 0], b_r.at[slot], in_column(one))
+            part = bbuf.at[slot, pl.ds(p * 256, 256)]
+            send(part, part, bp_s.at[p, 1], b_r.at[slot], in_column(two))
+
+    @pl.when(native)
+    def _():
+        bbuf[slot_at(0)] = vb[...]
+        spread_b()
+
+    @pl.when(jnp.logical_not(native))
+    def _():
+        bown[...] = vb[...]
+        slot = l * 4 + div(z, 2)
+        send(bown, bbuf.at[slot], bx_s, bx_r, dev(y, rem(z + 1, 8), h, half, c))
+
+    abuf[xi] = va[...]
+    for i, e in enumerate((4, 2, 6)):
+        send(abuf.at[xi], abuf.at[xi], a_s.at[i], a_r.at[xi], ring_dev(y, z, rem(xi + e, 8)))
+    send(abuf.at[xi], abuf.at[xi], a_s.at[3], a_r.at[xi], ring_dev(y, z, twin))
+
     wait(stats.at[pl.ds(0, 15)], st_r)
     total = stats[0]
     for i in range(1, 16):
@@ -102,44 +148,51 @@
     mean_a, mean_b = total[0:1, :], total[2:3, :]
     inv_a = lax.rsqrt(total[1:2, :] - mean_a * mean_a + epsilon)
     inv_b = lax.rsqrt(total[3:4, :] - mean_b * mean_b + epsilon)
-
-    half = rem(z, 2)
-    native = half == l
-    bslot = l * 4 + div(z, 2)
-    bbuf[8] = ((vb[...].astype(f32) - mean_b) * inv_b).astype(bf16)
-    for i, d in enumerate((2, 6, 1, 7)):
-        send(bbuf.at[8], bbuf.at[bslot], b_s.at[i], b_r.at[bslot], dev(y, rem(z + d, 8), h, half, c))
-    abuf[xi] = ((va[...].astype(f32) - mean_a) * inv_a).astype(bf16)
-    twin = xi + 1 - 2 * c
+    own_ab = h * 2 + c
+    astat[own_ab] = jnp.concatenate([mean_a, inv_a, mean_b, inv_b, jnp.zeros((4, 128), f32)], axis=0)
+    for e in range(1, 4):
+        to = rem(own_ab + e, 4)
+        send(astat.at[own_ab], astat.at[own_ab], ms_s, as_r.at[own_ab], ring_dev(y, z, l * 4 + to))
+
+    @pl.when(native)
+    def _():
+        own_q = div(z, 2)
+        bstat[own_q] = astat[own_ab]
+        for d in (1, 7, 2, 6, 3, 5, 4):
+            send(bstat.at[own_q], bstat.at[own_q], ms_s, bs_r.at[own_q], in_column(d))
+
+    @pl.when(native)
+    def _():
+        pass_b()
+
+    @pl.when(jnp.logical_not(native))
+    def _():
+        wait(bbuf.at[slot_at(0)], bx_r)
+        spread_b()
+
     for i, e in enumerate((4, 2, 6)):
-        send(abuf.at[xi], abuf.at[xi], a_s.at[i], a_r.at[xi], ring_dev(y, z, rem(xi + e, 8)))
-    send(abuf.at[xi], abuf.at[xi], a_s.at[3], a_r.at[xi], ring_dev(y, z, twin))
-
-    @pl.when(jnp.logical_not(native))
-    def _():
-        send(bbuf.at[8], bbuf.at[bslot], b_s.at[4], b_r.at[bslot], dev(y, z, h, half, c))
-
-    @pl.when(native)
-    def _():
-        bbuf[bslot] = bbuf[8]
-        for p, (frm, one, two) in enumerate(((6, 1, 2), (2, 7, 6))):
-            for k in range(2):
-                slot = k * 4 + div(rem(z + frm, 8), 2)
-                wait(bbuf.at[slot], b_r.at[slot])
-                send(bbuf.at[slot], bbuf.at[slot], bp_s.at[p, k, 0], b_r.at[slot], dev(y, rem(z + one, 8), h, l, c))
-                part = bbuf.at[slot, pl.ds(p * 256, 256)]
-                send(part, part, bp_s.at[p, k, 1], b_r.at[slot], dev(y, rem(z + two, 8), h, l, c))
-
-    def turn(slot):
-        aturn[rem(slot, 4), :, pl.ds(pl.multiple_of(div(slot, 4) * 512, 512), 512)] = abuf[slot].T
-
-    turn(xi)
-    for i, e in enumerate((2, 6, 4)):
         slot = rem(xi + e, 8)
         wait(abuf.at[slot], a_r.at[slot])
         send(abuf.at[slot], abuf.at[slot], a_s.at[4 + i], a_r.at[slot], ring_dev(y, z, twin))
-        turn(slot)
-    for e in (0, 2, 6, 4):
+
+    for e in range(1, 4):
+        wait(astat.at[rem(own_ab + e, 4)], as_r.at[rem(own_ab + e, 4)])
+
+    def turn(slot):
+        which = rem(slot, 4)
+        mean, inv = astat[which, 0:1, :], astat[which, 1:2, :]
+        normed = ((abuf[slot].astype(f32) - mean) * inv).astype(bf16)
+        anorm[slot] = normed
+        aturn[which, :, pl.ds(pl.multiple_of(div(slot, 4) * 512, 512), 512)] = normed.T
+
+    for e in (0, 4, 2, 6):
+        turn(rem(xi + e, 8))
+
+    @pl.when(jnp.logical_not(native))
+    def _():
+        pass_b()
+
+    for e in (0, 4, 2, 6):
         slot = rem(twin + e, 8)
         wait(abuf.at[slot], a_r.at[slot])
         turn(slot)
@@ -151,7 +204,7 @@
     over_in = (((1,), (0,)), ((), ()))
 
     def block(t):
-        ahead = jnp.where(native, (2, 6, 4, 0)[t], (3, 5, 1, 7)[t])
+        ahead = jnp.where(native, (0, 2, 4, 6)[t], (7, 5, 3, 1)[t])
         return div(rem(z + ahead, 8), 2)
 
     def along_y(e):
@@ -162,19 +215,20 @@
 
     def correlate(t):
         q = block(t)
-        for k in range(2):
-            if t < 2:
-                @pl.when(jnp.logical_not(native))
-                def _(k=k):
-                    wait(bbuf.at[k * 4 + q], b_r.at[k * 4 + q])
-            elif t == 2:
-                wait(bbuf.at[k * 4 + q], b_r.at[k * 4 + q])
-            else:
-                @pl.when(jnp.logical_not(native & (l == k)))
-                def _(k=k):
-                    wait(bbuf.at[k * 4 + q], b_r.at[k * 4 + q])
-
+        late = 1 - half
+        wait(bbuf.at[late * 4 + q], b_r.at[late * 4 + q])
+        if t == 2:
+            wait(bbuf.at[half * 4 + q], b_r.at[half * 4 + q])
+
+        @pl.when(jnp.logical_not(native) | (div(z, 2) != q))
+        def _():
+            wait(bstat.at[q], bs_r.at[q])
+
+        mean, inv = bstat[q, 2:3, :], bstat[q, 3:4, :]
         right = jnp.concatenate([bbuf[q], bbuf[4 + q]], axis=0)
+        right = ((right.astype(f32) - mean) * inv).astype(bf16)
+        bnorm[q] = right[:512]
+        bnorm[4 + q] = right[512:]
         left = jnp.concatenate([aturn[i] for i in range(4)], axis=0)
         part = lax.dot_general(left, right, over_in, preferred_element_type=f32)
         cwide[t] = part
@@ -256,67 +310,50 @@
             proj_a[i // 2] = proj_a[i // 2] + (sums[2:3, :] + sums[3:4, :])
         proj_b.append(total)
 
-    def in_column(d):
-        return dev(y, rem(z + d, 8), h, l, c)
-
     def back_columns(t):
         q = block(t)
-        for k in range(2):
-            back = lax.dot_general(side(abuf, k), gfull[q], over_in, preferred_element_type=f32)
-            back = back - bbuf[k * 4 + q].astype(f32) * proj_b[t]
-            if t < 2:
-                bkeep[t, k] = back
-            bsend[t, k] = back.astype(bf16)
-
-            if t < 2:
-                @pl.when(jnp.logical_not(native))
-                def _(k=k):
-                    send(bsend.at[t, k], bfull.at[t, k], fb_s.at[t, k], ff_r.at[t, k], in_column((1, 7)[t]))
-            elif t == 2:
-                @pl.when(native)
-                def _(k=k):
+        for j in range(2):
+            k = l if j == 0 else 1 - l
+            left = jnp.concatenate([anorm[k * 4 + i] for i in range(4)], axis=1)
+            back = lax.dot_general(left, gfull[q], over_in, preferred_element_type=f32)
+            back = back - bnorm[k * 4 + q].astype(f32) * proj_b[t]
+            if t != 2:
+                bkeep[min(t, 2), j] = back
+            bsend[t, j] = back.astype(bf16)
+
+            def act(off):
+                src = bsend.at[t, j]
+                sem = fb_s.at[t, j]
+                if off in (1, 7):
+                    i = 0 if off == 1 else 1
+                    send(src, bback.at[i], sem, fb_r.at[i], in_column(off))
+                if off in (3, 5):
+                    p = 0 if off == 3 else 1
+                    send(src, bfull.at[p], sem, ff_r.at[p], in_column((1, 7)[p]))
+                if off == 4:
                     for p, d in enumerate((2, 6)):
                         rows = pl.ds(256 - p * 256, 256)
-                        send(
-                            bsend.at[t, k, rows], bhalf.at[p, k, rows], fb_s.at[t, k], fh_r.at[p, k], in_column(d)
-                        )
-
-                @pl.when(jnp.logical_not(native))
-                def _(k=k):
-                    send(
-                        bsend.at[t, k], bback.at[0], fb_s.at[t, k], fb_r.at[0], dev(y, rem(z + 1, 8), h, jnp.int32(k), c)
-                    )
-            else:
-                @pl.when(native & (l == k))
-                def _(k=k):
-                    bback[4] = bsend[t, k]
-
-                @pl.when(native & (l != k))
-                def _(k=k):
-                    send(bsend.at[t, k], bback.at[4], fb_s.at[t, k], fb_r.at[4], dev(y, z, h, jnp.int32(k), c))
-
-                @pl.when(jnp.logical_not(native))
-                def _(k=k):
-                    send(
-                        bsend.at[t, k], bback.at[1], fb_s.at[t, k], fb_r.at[1], dev(y, rem(z + 7, 8), h, jnp.int32(k), c)
-                    )
-
-    def pass_back():
-        for p, d in enumerate((2, 6)):
-            for k in range(2):
-                rows = pl.ds(256 - p * 256, 256)
-                wait(bfull.at[p, k], ff_r.at[p, k])
-                wait(bhalf.at[p, k, rows], fh_r.at[p, k])
-                one = slice(256 - p * 256, 512 - p * 256)
-                other = slice(p * 256, 256 + p * 256)
-                bpass[p, k, other, :] = (bkeep[p, k, other, :] + bfull[p, k, other, :].astype(f32)).astype(bf16)
-                bpass[p, k, one, :] = (
-                    bkeep[p, k, one, :] + bfull[p, k, one, :].astype(f32) + bhalf[p, k, one, :].astype(f32)
-                ).astype(bf16)
-                send(
-                    bpass.at[p, k], bback.at[2 + p], fbp_s.at[p, k], fb_r.at[2 + p],
-                    dev(y, rem(z + d, 8), h, jnp.int32(k), c),
-                )
+                        send(bsend.at[t, j, rows], bhalf.at[p, rows], sem, fh_r.at[p], in_column(d))
+
+            @pl.when(native)
+            def _():
+                act(offs_on[t][j])
+
+            @pl.when(jnp.logical_not(native))
+            def _():
+                act(offs_off[t][j])
+
+    def pass_back(p):
+        d = (2, 6)[p]
+        keep = bkeep.at[jnp.where(native, (1, 2)[p], (2, 1)[p]), jnp.where(native, 0, 1)]
+        rows = pl.ds(256 - p * 256, 256)
+        wait(bfull.at[p], ff_r.at[p])
+        wait(bhalf.at[p, rows], fh_r.at[p])
+        one = slice(256 - p * 256, 512 - p * 256)
+        other = slice(p * 256, 256 + p * 256)
+        bpass[p, other, :] = (keep[other, :] + bfull[p, other, :].astype(f32)).astype(bf16)
+        bpass[p, one, :] = (keep[one, :] + bfull[p, one, :].astype(f32) + bhalf[p, one, :].astype(f32)).astype(bf16)
+        send(bpass.at[p], bback.at[2 + p], fbp_s.at[p], fb_r.at[2 + p], in_column(d))
 
     correlate(0)
     correlate(1)
@@ -355,9 +392,9 @@
     take_gradient(3)
     whole_g = jnp.concatenate([gfull[q] for q in range(4)], axis=1)
     for k in range(2):
-        back = lax.dot_general(side(bbuf, k), whole_g, over_cols, preferred_element_type=f32)
+        back = lax.dot_general(side(bnorm, k), whole_g, over_cols, preferred_element_type=f32)
         for i in range(4):
-            less = back[:, i * 128 : (i + 1) * 128] - abuf[k * 4 + i].astype(f32) * proj_a[i]
+            less = back[:, i * 128 : (i + 1) * 128] - anorm[k * 4 + i].astype(f32) * proj_a[i]
             akeep[k * 4 + i] = less
             asend[k * 4 + i] = less.astype(bf16)
     chip = l * 2 + h
@@ -365,7 +402,23 @@
         to = rem(chip + e, 4)
         send(asend.at[to * 2 + 1 - c], ain.at[to], fd_s.at[e], fd_r.at[to], ring_dev(y, z, twin))
 
+    @pl.when(native)
+    def _():
+        pass_back(0)
+
+    @pl.when(jnp.logical_not(native))
+    def _():
+        pass_back(1)
+
     back_columns(3)
+
+    @pl.when(native)
+    def _():
+        pass_back(1)
+
+    @pl.when(jnp.logical_not(native))
+    def _():
+        pass_back(0)
 
     for e in (2, 1, 3, 0):
         to = rem(chip + e, 4)
@@ -377,10 +430,6 @@
         else:
             aback[chip] = summed
 
-    @pl.when(native)
-    def _():
-        pass_back()
-
     for k in range(2):
         for p in range(2):
             @pl.when(jnp.logical_not(at_home & (c == k) & (rem(y, 2) == p)))
@@ -389,17 +438,20 @@
 
             co[p * 64 : (p + 1) * 64, k * 128 : (k + 1) * 128] = corrb[k, p]
 
+    acc = bkeep[0, jnp.where(native, 0, 1)]
     for i in range(4):
         wait(bback.at[i], fb_r.at[i])
-
-    @pl.when(jnp.logical_not(native))
-    def _():
-        wait(bback.at[4], fb_r.at[4])
-
-    acc = bback[0].astype(f32)
-    for i in range(1, 5):
         acc = acc + bback[i].astype(f32)
-    gb[...] = (acc * inv_b).astype(bf16)
+
+    @pl.when(native)
+    def _():
+        gb[...] = (acc * inv_b).astype(bf16)
+
+    @pl.when(jnp.logical_not(native))
+    def _():
+        wait(bown, bx_s)
+        bown[...] = acc.astype(bf16)
+        send(bown, bcross, bc_s, bc_r, dev(y, rem(z + 7, 8), h, 1 - l, c))
 
     for e in range(1, 4):
         frm = rem(chip + e, 4)
@@ -409,9 +461,20 @@
         acc = acc + aback[i].astype(f32)
     ga[...] = (acc * inv_a).astype(bf16)
 
+    @pl.when(jnp.logical_not(native))
+    def _():
+        wait(bcross, bc_r)
+        gb[...] = (bcross[...].astype(f32) * inv_b).astype(bf16)
+
+    @pl.when(native)
+    def _():
+        wait(stats.at[pl.ds(0, 10)], ms_s)
+
+    @pl.when(jnp.logical_not(native))
+    def _():
+        wait(stats.at[pl.ds(0, 3)], ms_s)
+
     wait(stats.at[pl.ds(0, 15)], st_s)
-    for i in range(4):
-        wait(bbuf.at[8], b_s.at[i])
     for i in range(7):
         wait(abuf.at[xi], a_s.at[i])
     for e in range(4):
@@ -421,15 +484,14 @@
 
     @pl.when(jnp.logical_not(native))
     def _():
-        wait(bbuf.at[8], b_s.at[4])
-
-    @pl.when(native)
-    def _():
-        for p in range(2):
-            for k in range(2):
-                wait(bbuf.at[8], bp_s.at[p, k, 0])
-                wait(bbuf.at[8, pl.ds(0, 256)], bp_s.at[p, k, 1])
-                wait(bpass.at[p, k], fbp_s.at[p, k])
+        wait(bown, bc_s)
+
+    for i in range(4):
+        wait(bbuf.at[0], b_s.at[i])
+    for p in range(2):
+        wait(bbuf.at[0], bp_s.at[p, 0])
+        wait(bbuf.at[0, pl.ds(0, 256)], bp_s.at[p, 1])
+        wait(bpass.at[p], fbp_s.at[p])
 
     for t in range(4):
         wait(crecv.at[t, pl.ds(0, 5)], c_s.at[t])
@@ -440,10 +502,19 @@
         def _(t=t):
             wait(ctile.at[t], o_s.at[t])
 
-        for k in range(2):
-            @pl.when((jnp.logical_not(native)) | (t == 2) | ((t == 3) & (l != k)))
-            def _(k=k, t=t):
-                wait(bsend.at[t, k], fb_s.at[t, k])
+        for j in range(2):
+            goes_on = offs_on[t][j] not in (0, 2, 6)
+            goes_off = offs_off[t][j] not in (0, 2, 6)
+            if goes_on and goes_off:
+                wait(bsend.at[t, j], fb_s.at[t, j])
+            elif goes_on:
+                @pl.when(native)
+                def _(t=t, j=j):
+                    wait(bsend.at[t, j], fb_s.at[t, j])
+            elif goes_off:
+                @pl.when(jnp.logical_not(native))
+                def _(t=t, j=j):
+                    wait(bsend.at[t, j], fb_s.at[t, j])
 
 
 def body(view_a, view_b):
@@ -468,8 +539,12 @@
         scratch_shapes=[
             pltpu.VMEM((8, 128), f32),
             pltpu.VMEM((16, 8, 128), f32),
+            pltpu.VMEM((4, 8, 128), f32),
+            pltpu.VMEM((4, 8, 128), f32),
             pltpu.VMEM((8, rows, 128), bf16),
-            pltpu.VMEM((9, rows, 128), bf16),
+            pltpu.VMEM((8, rows, 128), bf16),
+            pltpu.VMEM((8, rows, 128), bf16),
+            pltpu.VMEM((8, rows, 128), bf16),
             pltpu.VMEM((4, 128, 1024), bf16),
             pltpu.VMEM((4, 512, 128), f32),
             pltpu.VMEM((4, 512, 128), bf16),
@@ -480,21 +555,23 @@
             pltpu.VMEM((4, 8, 80, 128), bf16),
             pltpu.VMEM((4, 512, 128), bf16),
             pltpu.VMEM((4, 2, rows, 128), bf16),
-            pltpu.VMEM((2, 2, rows, 128), f32),
-            pltpu.VMEM((2, 2, rows, 128), bf16),
-            pltpu.VMEM((2, 2, rows, 128), bf16),
-            pltpu.VMEM((2, 2, rows, 128), bf16),
-            pltpu.VMEM((5, rows, 128), bf16),
+            pltpu.VMEM((3, 2, rows, 128), f32),
+            pltpu.VMEM((2, rows, 128), bf16),
+            pltpu.VMEM((2, rows, 128), bf16),
+            pltpu.VMEM((2, rows, 128), bf16),
+            pltpu.VMEM((4, rows, 128), bf16),
+            pltpu.VMEM((rows, 128), bf16),
+            pltpu.VMEM((rows, 128), bf16),
             pltpu.VMEM((8, rows, 128), bf16),
             pltpu.VMEM((8, rows, 128), f32),
             pltpu.VMEM((4, rows, 128), bf16),
             pltpu.VMEM((4, rows, 128), bf16),
             pltpu.VMEM((4, rows, 128), bf16),
-            dma, dma,
-            dma((7,)), dma((8,)), dma((5,)), dma((8,)), dma((2, 2, 2)),
+            dma, dma, dma, dma((4,)), dma((4,)),
+            dma((7,)), dma((8,)), dma((4,)), dma((8,)), dma((2, 2)),
             dma((4,)), dma((4,)), dma((4,)), dma((4,)), dma((4,)), dma((2, 2)), dma((4,)), dma((4,)), dma((4,)),
-            dma((4, 2)), dma((2, 2)), dma((2, 2)), dma((2, 2)), dma((5,)),
-            dma((4,)), dma((4,)), dma((4,)), dma((4,)),
+            dma((4, 2)), dma((2,)), dma((2,)), dma((2,)), dma((4,)),
+            dma((4,)), dma((4,)), dma((4,)), dma((4,)), dma, dma, dma, dma,
         ],
         compiler_params=pltpu.CompilerParams(
             collective_id=0, has_side_effects=True, vmem_limit_bytes=40 * 2**20

time: 88.2 us -> 82 us (0.930)
  the two profiles are of different devices: /device:TPU:16 before, /device:TPU:64 now
where the time goes in v3:
time: 82 us; the launch traced here: 81.9 us
  Pallas kernels  77.5 us (95%)
  local copies, waits for them, and re-layouts  3.77 us (5%)
    pallas_call x1, Pallas kernels, body(): pl.pallas_call(call, name='barlow', out_shape=(jax.ShapeDtypeStruct((rows...  77.5 us
    unnamed x7, local copies, waits for them, and re-layouts  3.77 us

profile of v3, /device:TPU:64, one launch (start us, length us, event | category | flops | bytes accessed | tf_op | source)
XLA Modules:
  0.0 81.9 jit_solution(12898995097554783493)
XLA Ops:
  0.6 0.0 copy-start
  0.6 0.9 %copy-done = bf16[512,128]{1,0:T(8,128)(2,1)S(1)} copy-done((bf16[512,128]{1,0:T(8,128)(2,1)S(1)}, bf16[512,128]{1,0:T(8,128)(2,1)}, u32[]{:S(2)}) %copy-start) | copy-done | bytes 131096
  1.5 0.0 copy-start.1
  1.5 0.9 %copy-done.1 = bf16[512,128]{1,0:T(8,128)(2,1)S(1)} copy-done((bf16[512,128]{1,0:T(8,128)(2,1)S(1)}, bf16[512,128]{1,0:T(8,128)(2,1)}, u32[]{:S(2)}) %copy-start.1) | copy-done | bytes 131096
  2.4 77.5 %barlow.1 = (bf16[512,128]{1,0:T(8,128)(2,1)S(1)}, bf16[512,128]{1,0:T(8,128)(2,1)S(1)}, f32[128,256]{1,0:T(8,128)S(1)}) custom-call(bf16[512,128]{1,0:T(8,128)(2,1)S(1)} %copy-done, bf16[512,128]{1,0:T(8,128)(2,1)S(1)} %copy-done.1), custom_call_target="tpu_custom_call" | custom-call | tf_op jit(solution)/shard_map/barlow/pallas_call | solution.py:529
  79.9 0.7 copy.8
  80.6 0.7 copy.9
  81.2 0.7 copy.10
Async XLA Ops:
  0.6 0.9 %copy-start = (bf16[512,128]{1,0:T(8,128)(2,1)S(1)}, bf16[512,128]{1,0:T(8,128)(2,1)}, u32[]{:S(2)}) copy-start(bf16[512,128]{1,0:T(8,128)(2,1)} %args_0_.4) | copy-start | bytes 393220
  1.5 0.9 %copy-start.1 = (bf16[512,128]{1,0:T(8,128)(2,1)S(1)}, bf16[512,128]{1,0:T(8,128)(2,1)}, u32[]{:S(2)}) copy-start(bf16[512,128]{1,0:T(8,128)(2,1)} %args_1_.4) | copy-start | bytes 393220

commit v4 on v3

--- a/solution.py
+++ b/solution.py
@@ -20,14 +20,18 @@
     return lax.rem(a, jnp.int32(n))
 
 
+straight_c = ()
+straight_g = ()
+
 offs_on = ((0, 1), (2, 3), (4, 5), (6, 7))
 offs_off = ((7, 0), (5, 6), (3, 4), (1, 2))
 
 
 def kernel(
     pairs,
-    va, vb,
+    view_a, view_b,
     ga, gb, co,
+    va, vb, in_s,
     stat_own, stats, astat, bstat, abuf, bbuf, anorm, bnorm, aturn, cwide, cnarrow, crecv, cpass, ctile, corrb,
     gbuf, gfull, bsend, bkeep, bfull, bhalf, bpass, bback, bown, bcross, asend, akeep, ain, apass, aback,
     st_s, st_r, ms_s, as_r, bs_r, a_s, a_r, b_s, b_r, bp_s, c_s, cp_s, cp_r, c_r, o_s, o_r, g_s, gp_r, g_r,
@@ -68,6 +72,9 @@
 
     at_home = (rem(y, 2) == l) & (h == l) & (div(y, 2) == h * 2 + c)
 
+    pltpu.make_async_copy(view_a, va, in_s.at[0]).start()
+    pltpu.make_async_copy(view_b, vb, in_s.at[1]).start()
+
     barrier = pltpu.get_barrier_semaphore()
 
     def greet(to):
@@ -86,6 +93,8 @@
         def _(q=q):
             greet(corr_from(q // 2, q % 2))
 
+    wait(va, in_s.at[0])
+    wait(vb, in_s.at[1])
     wide_a = va[...].astype(f32)
     wide_b = vb[...].astype(f32)
     stat_own[0:1, :] = jnp.sum(wide_a, axis=0, keepdims=True)
@@ -238,6 +247,10 @@
             piece = cnarrow.at[t, pl.ds(pl.multiple_of(rem(y + e, 8) * 64 + lo, 32), n)]
             send(piece, crecv.at[t, slot, pl.ds(lo, n)], c_s.at[t], sem, along_y(to))
 
+        if t in straight_c:
+            for e in (4, 3, 5, 2, 6, 1, 7):
+                go(e, e, e, c_r.at[t])
+            return
         go(3, 1, 2, cp_r.at[t])
         go(5, 7, 3, cp_r.at[t])
         go(4, 6, 4, cp_r.at[t], 0, 32)
@@ -246,6 +259,8 @@
         go(7, 7, 1, c_r.at[t])
 
     def pass_partial(t):
+        if t in straight_c:
+            return
         wait(crecv.at[t, pl.ds(0, 3)], cp_r.at[t])
         up = cwide[t, rows_of(rem(y + 2, 8)), :] + crecv[t, 2].astype(f32)
         cpass[t, 0, 0:32, :] = up[:32].astype(bf16)
@@ -258,9 +273,10 @@
 
     def differentiate(t):
         q = block(t)
-        wait(crecv.at[t, pl.ds(0, 4)], c_r.at[t])
+        straight = t in straight_c
+        wait(crecv.at[t, pl.ds(0, 7 if straight else 4)], c_r.at[t])
         corr = cwide[t, rows_of(y), :]
-        for i in (0, 1, 6, 7):
+        for i in range(1, 8) if straight else (0, 1, 6, 7):
             corr = corr + crecv[t, i].astype(f32)
         corr = corr / pairs
         ctile[q] = corr
@@ -282,12 +298,18 @@
         terms.append(jnp.zeros((12, 128), f32))
         gbuf[q, y, 0:64, :] = grad
         gbuf[q, y, 64:80, :] = jnp.concatenate(terms, axis=0).astype(bf16)
+        if t in straight_g:
+            for e in (4, 3, 5, 2, 6, 1, 7):
+                send(gbuf.at[q, y], gbuf.at[q, y], g_s.at[t], g_r.at[t], along_y(e))
+            return
         send(gbuf.at[q, y], gbuf.at[q, y], g_s.at[t], gp_r.at[t], along_y(2))
         send(gbuf.at[q, y], gbuf.at[q, y], g_s.at[t], gp_r.at[t], along_y(6))
         send(gbuf.at[q, y], gbuf.at[q, y], g_s.at[t], g_r.at[t], along_y(1))
         send(gbuf.at[q, y], gbuf.at[q, y], g_s.at[t], g_r.at[t], along_y(7))
 
     def pass_gradient(t):
+        if t in straight_g:
+            return
         q = block(t)
         wait(gbuf.at[q, pl.ds(0, 2)], gp_r.at[t])
         for frm, one, two, lo, n in ((6, 1, 2, 0, 48), (2, 7, 6, 48, 32)):
@@ -301,7 +323,7 @@
 
     def take_gradient(t):
         q = block(t)
-        wait(gbuf.at[q, pl.ds(0, 5)], g_r.at[t])
+        wait(gbuf.at[q, pl.ds(0, 7 if t in straight_g else 5)], g_r.at[t])
         total = jnp.zeros((1, 128), f32)
         for i in range(8):
             gfull[q, i * 64 : (i + 1) * 64, :] = gbuf[q, i, 0:64, :]
@@ -494,8 +516,9 @@
         wait(bpass.at[p], fbp_s.at[p])
 
     for t in range(4):
-        wait(crecv.at[t, pl.ds(0, 5)], c_s.at[t])
-        wait(crecv.at[t, pl.ds(0, 2)], cp_s.at[t])
+        wait(crecv.at[t, pl.ds(0, 7 if t in straight_c else 5)], c_s.at[t])
+        if t not in straight_c:
+            wait(crecv.at[t, pl.ds(0, 2)], cp_s.at[t])
         wait(gbuf.at[t, pl.ds(0, 7)], g_s.at[t])
 
         @pl.when(jnp.logical_not(at_home & (div(y, 2) == t)))
@@ -526,7 +549,7 @@
     def call(*args):
         return kernel(float(pairs), *args)
 
-    return pl.pallas_call(
+    results = pl.pallas_call(
         call,
         name="barlow",
         out_shape=(
@@ -534,9 +557,12 @@
             jax.ShapeDtypeStruct((rows, cols), bf16),
             jax.ShapeDtypeStruct((128, 256), f32),
         ),
-        in_specs=[vmem, vmem],
+        in_specs=[pl.BlockSpec(memory_space=pltpu.HBM)] * 2,
         out_specs=(vmem, vmem, vmem),
         scratch_shapes=[
+            pltpu.VMEM((rows, cols), bf16),
+            pltpu.VMEM((rows, cols), bf16),
+            dma((2,)),
             pltpu.VMEM((8, 128), f32),
             pltpu.VMEM((16, 8, 128), f32),
             pltpu.VMEM((4, 8, 128), f32),
@@ -574,9 +600,29 @@
             dma((4,)), dma((4,)), dma((4,)), dma((4,)), dma, dma, dma, dma,
         ],
         compiler_params=pltpu.CompilerParams(
-            collective_id=0, has_side_effects=True, vmem_limit_bytes=40 * 2**20
+            collective_id=0, has_side_effects=True, vmem_limit_bytes=60 * 2**20
         ),
     )(view_a, view_b)
+
+    def place(grad_a, grad_b, corr, out_a, out_b, out_c, sems):
+        copies = [
+            pltpu.make_async_copy(src, dst, sems.at[i])
+            for i, (src, dst) in enumerate(((grad_a, out_a), (grad_b, out_b), (corr, out_c)))
+        ]
+        for copy in copies:
+            copy.start()
+        for copy in copies:
+            copy.wait()
+
+    anywhere = pl.BlockSpec(memory_space=pl.ANY)
+    return pl.pallas_call(
+        place,
+        name="place",
+        out_shape=tuple(jax.ShapeDtypeStruct(r.shape, r.dtype) for r in results),
+        in_specs=[vmem] * 3,
+        out_specs=(anywhere,) * 3,
+        scratch_shapes=[dma((3,))],
+    )(*results)
 
 
 def solution(mesh):

time: 82 us -> 80.9 us (0.987)
  local copies, waits for them, and re-layouts: 3.77 us -> 0 us
  Pallas kernels: 77.5 us -> 80.1 us
    unnamed x7 -> x0, local copies, waits for them, and re-layouts: 3.77 us -> none
    pallas_call x0 -> x1, Pallas kernels: none -> 1.8 us  [body(): pl.pallas_call(place, name='place', out_shape=tuple((jax.ShapeDtypeStruct...]
where the time goes in v4:
time: 80.9 us; the launch traced here: 80.7 us
  Pallas kernels  80.1 us (99%)
    pallas_call x1, Pallas kernels, body(): pl.pallas_call(call, name='barlow', out_shape=(jax.ShapeDtypeStruct((rows...  78.3 us
    pallas_call x1, Pallas kernels, body(): pl.pallas_call(place, name='place', out_shape=tuple((jax.ShapeDtypeStruct...  1.8 us

profile of v4, /device:TPU:64, one launch (start us, length us, event | category | flops | bytes accessed | tf_op | source)
XLA Modules:
  0.0 80.7 jit_solution(8308763672198754128)
XLA Ops:
  0.6 78.3 %barlow.1 = (bf16[512,128]{1,0:T(8,128)(2,1)}, bf16[512,128]{1,0:T(8,128)(2,1)}, f32[128,256]{1,0:T(8,128)}) custom-call(bf16[512,128]{1,0:T(8,128)(2,1)} %args_0_.4, bf16[512,128]{1,0:T(8,128)(2,1)} %args_1_.4), custom_call_target="tpu_custom_call" | custom-call | tf_op jit(solution)/shard_map/barlow/pallas_call | solution.py:552
  78.9 1.8 %place.1 = (bf16[512,128]{1,0:T(8,128)(2,1)}, bf16[512,128]{1,0:T(8,128)(2,1)}, f32[128,256]{1,0:T(8,128)}) custom-call(bf16[512,128]{1,0:T(8,128)(2,1)} %get-tuple-element.6.grad_a, bf16[512,128]{1,0:T(8,128)(2,1)} %get-tuple-element.7.grad_b, f32[128,256]{1,0:T(8,128)} %get-tuple-element.8.corr), custom_call_target="tpu_custom_call" | custom-call | tf_op jit(solution)/shard_map/place/pallas_call | solution.py:618

commit v5 on v4

--- a/solution.py
+++ b/solution.py
@@ -149,6 +149,15 @@
         send(abuf.at[xi], abuf.at[xi], a_s.at[i], a_r.at[xi], ring_dev(y, z, rem(xi + e, 8)))
     send(abuf.at[xi], abuf.at[xi], a_s.at[3], a_r.at[xi], ring_dev(y, z, twin))
 
+    @pl.when(native)
+    def _():
+        pass_b()
+
+    @pl.when(jnp.logical_not(native))
+    def _():
+        wait(bbuf.at[slot_at(0)], bx_r)
+        spread_b()
+
     wait(stats.at[pl.ds(0, 15)], st_r)
     total = stats[0]
     for i in range(1, 16):
@@ -169,15 +178,6 @@
         bstat[own_q] = astat[own_ab]
         for d in (1, 7, 2, 6, 3, 5, 4):
             send(bstat.at[own_q], bstat.at[own_q], ms_s, bs_r.at[own_q], in_column(d))
-
-    @pl.when(native)
-    def _():
-        pass_b()
-
-    @pl.when(jnp.logical_not(native))
-    def _():
-        wait(bbuf.at[slot_at(0)], bx_r)
-        spread_b()
 
     for i, e in enumerate((4, 2, 6)):
         slot = rem(xi + e, 8)
@@ -400,17 +400,6 @@
     take_gradient(2)
     back_columns(2)
 
-    for q in range(4):
-        stay = at_home & (div(y, 2) == q)
-
-        @pl.when(stay)
-        def _(q=q):
-            corrb[c, rem(y, 2)] = ctile[q]
-
-        @pl.when(jnp.logical_not(stay))
-        def _(q=q):
-            send(ctile.at[q], corrb.at[c, rem(y, 2)], o_s.at[q], o_r.at[c, rem(y, 2)], corr_to(q))
-
     take_gradient(3)
     whole_g = jnp.concatenate([gfull[q] for q in range(4)], axis=1)
     for k in range(2):
@@ -441,6 +430,17 @@
     @pl.when(jnp.logical_not(native))
     def _():
         pass_back(0)
+
+    for q in range(4):
+        stay = at_home & (div(y, 2) == q)
+
+        @pl.when(stay)
+        def _(q=q):
+            corrb[c, rem(y, 2)] = ctile[q]
+
+        @pl.when(jnp.logical_not(stay))
+        def _(q=q):
+            send(ctile.at[q], corrb.at[c, rem(y, 2)], o_s.at[q], o_r.at[c, rem(y, 2)], corr_to(q))
 
     for e in (2, 1, 3, 0):
         to = rem(chip + e, 4)

time: 80.9 us -> 80.6 us (level)
  no operation moved by 1% of the time
where the time goes in v5:
time: 80.6 us; the launch traced here: 80.5 us
  Pallas kernels  79.8 us (99%)
    pallas_call x1, Pallas kernels, body(): pl.pallas_call(call, name='barlow', out_shape=(jax.ShapeDtypeStruct((rows...  78 us
    pallas_call x1, Pallas kernels, body(): pl.pallas_call(place, name='place', out_shape=tuple((jax.ShapeDtypeStruct...  1.8 us

profile of v5, /device:TPU:64, one launch (start us, length us, event | category | flops | bytes accessed | tf_op | source)
XLA Modules:
  0.0 80.5 jit_solution(14186858674631355993)
XLA Ops:
  0.6 78.0 %barlow.1 = (bf16[512,128]{1,0:T(8,128)(2,1)}, bf16[512,128]{1,0:T(8,128)(2,1)}, f32[128,256]{1,0:T(8,128)}) custom-call(bf16[512,128]{1,0:T(8,128)(2,1)} %args_0_.4, bf16[512,128]{1,0:T(8,128)(2,1)} %args_1_.4), custom_call_target="tpu_custom_call" | custom-call | tf_op jit(solution)/shard_map/barlow/pallas_call | solution.py:552
  78.7 1.8 %place.1 = (bf16[512,128]{1,0:T(8,128)(2,1)}, bf16[512,128]{1,0:T(8,128)(2,1)}, f32[128,256]{1,0:T(8,128)}) custom-call(bf16[512,128]{1,0:T(8,128)(2,1)} %get-tuple-element.6.grad_a, bf16[512,128]{1,0:T(8,128)(2,1)} %get-tuple-element.7.grad_b, f32[128,256]{1,0:T(8,128)} %get-tuple-element.8.corr), custom_call_target="tpu_custom_call" | custom-call | tf_op jit(solution)/shard_map/place/pallas_call | solution.py:618

commit v6 on v5

--- a/solution.py
+++ b/solution.py
@@ -401,6 +401,7 @@
     back_columns(2)
 
     take_gradient(3)
+    back_columns(3)
     whole_g = jnp.concatenate([gfull[q] for q in range(4)], axis=1)
     for k in range(2):
         back = lax.dot_general(side(bnorm, k), whole_g, over_cols, preferred_element_type=f32)
@@ -420,8 +421,6 @@
     @pl.when(jnp.logical_not(native))
     def _():
         pass_back(1)
-
-    back_columns(3)
 
     @pl.when(native)
     def _():

time: 80.6 us -> 79.3 us (0.984)
  Pallas kernels: 79.8 us -> 78.5 us
    pallas_call x1, Pallas kernels: 78 us -> 76.7 us  [body(): pl.pallas_call(call, name='barlow', out_shape=(jax.ShapeDtypeStruct((rows...]
where the time goes in v6:
time: 79.3 us; the launch traced here: 79.1 us
  Pallas kernels  78.5 us (99%)
    pallas_call x1, Pallas kernels, body(): pl.pallas_call(call, name='barlow', out_shape=(jax.ShapeDtypeStruct((rows...  76.7 us
    pallas_call x1, Pallas kernels, body(): pl.pallas_call(place, name='place', out_shape=tuple((jax.ShapeDtypeStruct...  1.8 us

profile of v6, /device:TPU:64, one launch (start us, length us, event | category | flops | bytes accessed | tf_op | source)
XLA Modules:
  0.0 79.1 jit_solution(5284121466072627646)
XLA Ops:
  0.6 76.7 %barlow.1 = (bf16[512,128]{1,0:T(8,128)(2,1)}, bf16[512,128]{1,0:T(8,128)(2,1)}, f32[128,256]{1,0:T(8,128)}) custom-call(bf16[512,128]{1,0:T(8,128)(2,1)} %args_0_.4, bf16[512,128]{1,0:T(8,128)(2,1)} %args_1_.4), custom_call_target="tpu_custom_call" | custom-call | tf_op jit(solution)/shard_map/barlow/pallas_call | solution.py:551
  77.3 1.8 %place.1 = (bf16[512,128]{1,0:T(8,128)(2,1)}, bf16[512,128]{1,0:T(8,128)(2,1)}, f32[128,256]{1,0:T(8,128)}) custom-call(bf16[512,128]{1,0:T(8,128)(2,1)} %get-tuple-element.6.grad_a, bf16[512,128]{1,0:T(8,128)(2,1)} %get-tuple-element.7.grad_b, f32[128,256]{1,0:T(8,128)} %get-tuple-element.8.corr), custom_call_target="tpu_custom_call" | custom-call | tf_op jit(solution)/shard_map/place/pallas_call | solution.py:617
